TPU v7x, 512 devices: a whole 4x8x8 slice. The times are simulated.
512 devices in a mesh: tm: 32 (over x, y), scen: 16 (over z, core).
Axes of the slice: x: 4, y: 8, z: 8, core: 2. Of those that a mesh axis runs over, the one named last changes fastest.
Arguments:
- closed_loop: float32 [1024, 96, 96], P('tm'), may hold values from -1 to 1
- gains: float32 [1024, 48, 96], P('tm'), may hold values from -0.625 to 0.625
- feedforward: float32 [1024, 48], P('tm'), may hold values from -6 to 6
- drift_terms: float32 [1024, 96], P('tm'), may hold values from -0.3 to 0.3
- initial_states: float32 [96, 1024], P(None, ('tm', 'scen')), may hold values from -6 to 6
Outputs:
- states: float32 [1024, 96, 1024], P(('tm', 'scen'))
- controls: float32 [1024, 48, 1024], P(('tm', 'scen'))
All inputs are finite; a program needn't handle non-finite values.
Results may differ from a plain program's by a relative error of at most 0.0003.
Values sent between devices are 32-bit elements; how exact they have to be, the bound alone decides.
No kernel may reach another device: no remote copies, remote signals or barrier semaphores. Data moves between devices by JAX's collectives and lax.ppermute only.
A program may use at most 64 MiB of HBM per device.

v0:
```python
import jax
import jax.numpy as jnp
from jax import lax
from jax.sharding import PartitionSpec as P

highest = lax.Precision.HIGHEST


def copy_for_each(array, axis):
    copies = jnp.broadcast_to(array, (lax.axis_size(axis), *array.shape))
    return lax.all_to_all(copies, axis, split_axis=0, concat_axis=0, tiled=True)


def joined_along(parts, dim):
    parts = jnp.moveaxis(parts, 0, dim)
    dims = parts.shape
    return parts.reshape(*dims[:dim], dims[dim] * dims[dim + 1], *dims[dim + 2 :])


def gathered_copies(array, axis, dim):
    parts = copy_for_each(array, axis)
    return joined_along(parts, dim)


def gathered_once(array, axis):
    leaves = jax.tree.leaves(array)
    turns = sorted(range(len(leaves)), key=lambda k: -leaves[k].size)
    width = (1, *leaves[turns[0]].shape)[-1]
    lines = [
        jnp.pad(leaves[k].reshape(-1), (0, -leaves[k].size % width)).reshape(-1, width)
        for k in turns
    ]
    both, at, found = (copy_for_each(jnp.concatenate(lines), axis), 0, {})
    for k, line in zip(turns, lines):
        share = both[:, at : at + len(line)].reshape(len(both), -1)
        found[k] = share[:, : leaves[k].size].reshape(-1, *leaves[k].shape)
        at += len(line)
    numbers = iter(range(len(leaves)))
    return jax.tree.map(lambda _: found[next(numbers)], array)


def joined_by_halves(pieces, combine):
    while len(jax.tree.leaves(pieces)[0]) > 1:
        pieces = jax.vmap(combine)(
            *(jax.tree.map(lambda part: part[side::2], pieces) for side in (0, 1))
        )
    return jax.tree.map(lambda part: part[0], pieces)


def carried_in(array, axis, combine, identity):
    length, index = (lax.axis_size(axis), lax.axis_index(axis))
    passed = jnp.arange(length) < index

    def kept(part, zero, own):
        part = jnp.where(
            passed.reshape(-1, *(1 for _ in own.shape)), part, jnp.asarray(zero, own.dtype)
        )
        return part

    pieces = gathered_once(array, axis)
    return joined_by_halves(jax.tree.map(kept, pieces, identity, array), combine)


def compose(earlier_maps, following_maps):
    first_matrix, first_offset = earlier_maps
    second_matrix, second_offset = following_maps
    matrix = jnp.einsum("tij,tjk->tik", second_matrix, first_matrix, precision=highest)
    shift_amount_term = (
        jnp.einsum("tij,tj->ti", second_matrix, first_offset, precision=highest) + second_offset
    )
    return (matrix, shift_amount_term)


def join_maps(earlier_map, following_map):
    matrix = jnp.dot(following_map[0], earlier_map[0], precision=highest)
    shift_amount_term = (
        jnp.dot(following_map[0], earlier_map[1], precision=highest) + following_map[1]
    )
    return (matrix, shift_amount_term)


def body(closed_loop, gains, feedforward, drift_terms, initial_states):
    vector_dimension = closed_loop.shape[1]
    prefix, offsets = lax.associative_scan(compose, (closed_loop, drift_terms))
    summary = (prefix[-1], offsets[-1])
    identity_map = jnp.eye(vector_dimension, dtype=jnp.float32)
    onset_positions = gathered_copies(initial_states, "tm", 1)
    empty_offset = jnp.zeros((vector_dimension,), jnp.float32)
    before_block = carried_in(summary, "tm", join_maps, (identity_map, empty_offset))
    entry_states = (
        jnp.dot(before_block[0], onset_positions, precision=highest) + before_block[1][:, None]
    )
    lead_maps = jnp.concatenate([identity_map[None], prefix[:-1]], axis=0)
    lead_offsets = jnp.concatenate(
        [jnp.zeros((1, vector_dimension), jnp.float32), offsets[:-1]], axis=0
    )
    states = (
        jnp.einsum("tij,js->sit", lead_maps, entry_states, precision=highest)
        + jnp.transpose(lead_offsets)[None]
    )
    controls = jnp.transpose(feedforward)[None] - jnp.einsum(
        "tai,sit->sat", gains, states, precision=highest
    )
    moved_states, moved_controls = (
        lax.all_to_all(states, "tm", split_axis=0, concat_axis=2, tiled=True),
        lax.all_to_all(controls, "tm", split_axis=0, concat_axis=2, tiled=True),
    )
    return (moved_states, moved_controls)


def solution(mesh):
    return jax.shard_map(
        body,
        mesh=mesh,
        in_specs=(
            P("tm", None, None),
            P("tm", None, None),
            P("tm", None),
            P("tm", None),
            P(None, ("tm", "scen")),
        ),
        out_specs=(P(("tm", "scen"), None, None), P(("tm", "scen"), None, None)),
        check_vma=False,
    )
```

profile of v0, /device:TPU:448, one launch (start us, length us, event | category | flops | bytes accessed | tf_op | source)
XLA Modules:
  0.0 187.2 jit_solution(5599669404182471864)
XLA Ops:
  0.6 2.9 %fusion.15 = f32[16,96,96]{1,2,0:T(8,128)S(1)} fusion(f32[32,96,96]{2,1,0:T(8,128)} %param.5), kind=kOutput, calls=%fused_computation.21 | convolution fusion | flops 169869312 | bytes 1769472 | tf_op jit(solution)/shard_map/tij,tjk->tik/dot_general | solution.py:67
  3.5 0.5 fusion.28
  4.0 0.3 fusion.41
  4.4 0.2 fusion.54
  5.0 0.2 copy-done.7
  5.3 0.3 fusion.47
  5.8 0.5 fusion.34
  6.3 0.8 add.134
  7.1 3.4 %pad.69 = f32[16,96,96]{1,2,0:T(8,128)} pad(f32[8,96,96]{1,2,0:T(8,128)S(1)} %pad_maximum_fusion.1, f32[]{:T(128)} %constant.5.clone.1), padding=0_1_1x0_0_0x0_0_0 | pad | bytes 884740 | tf_op jit(solution)/shard_map/pad | solution.py:84
  10.5 5.4 %pad.70 = f32[16,96,96]{1,2,0:T(8,128)} pad(f32[8,96,96]{1,2,0:T(8,128)} %add.134, f32[]{:T(128)} %constant.5.clone.1), padding=1_0_1x0_0_0x0_0_0 | pad | bytes 884740 | tf_op jit(solution)/shard_map/pad | solution.py:84
  15.9 1.5 add.135
  17.4 0.9 copy-done.4
  18.2 2.4 %convolution_bitcast_fusion.1 = f32[15,96,96]{1,2,0:T(8,128)} fusion(f32[16,96,96]{1,2,0:T(8,128)S(1)} %add.135, f32[32,96,96]{2,1,0:T(8,128)S(1)} %copy-done.1), kind=kOutput, calls=%fused_computation.8 | convolution fusion | flops 159252480 | bytes 2076672 | tf_op jit(solution)/shard_map/tij,tjk->tik/dot_general | solution.py:67
  20.7 9.7 %pad.72 = f32[32,96,96]{1,2,0:T(8,128)} pad(f32[16,96,96]{1,2,0:T(8,128)} %copy-done.4, f32[]{:T(128)} %constant.5.clone.1), padding=1_0_1x0_0_0x0_0_0 | pad | bytes 1769476 | tf_op jit(solution)/shard_map/pad | solution.py:84
  30.3 0.6 slice.246
  30.9 0.6 slice.247
  31.6 2.6 %fusion.20 = f32[16,1,96]{2,1,0:T(1,128)} fusion(f32[16,96,1]{1,2,0:T(1,128)} %bitcast.139, f32[32,96,96]{2,1,0:T(8,128)S(1)} %copy-done.1), kind=kOutput, calls=%fused_computation.26 | convolution fusion | flops 1769472 | bytes 798720 | tf_op jit(solution)/shard_map/tij,tj->ti/dot_general | solution.py:69
  34.2 0.8 copy.99
  35.0 0.8 copy.80
  37.7 0.3 convolution_add_fusion.1
  38.5 0.3 convolution_add_fusion
  40.7 1.2 pad_maximum_fusion
  41.9 6.1 %pad.71 = f32[32,96,96]{1,2,0:T(8,128)} pad(f32[16,96,96]{1,2,0:T(8,128)S(1)} %pad_maximum_fusion, f32[]{:T(128)} %constant.5.clone.1), padding=0_1_1x0_0_0x0_0_0 | pad | bytes 1769476 | tf_op jit(solution)/shard_map/pad | solution.py:84
  48.1 1.3 fusion.23
  49.5 0.3 pad.81
  49.8 0.3 pad.82
  50.1 0.8 add_bitcast_fusion.1
  51.1 1.3 broadcast_in_dim.36
  52.4 10.0 %all-to-all-start = ((f32[32,97,96]{1,2,0:T(8,128)}), f32[32,97,96]{1,2,0:T(8,128)S(1)}, u32[]{:S(2)}, u32[]{:S(2)}) async-start(f32[32,97,96]{1,2,0:T(8,128)} %broadcast_in_dim.36), calls=%async_computation | async-start | bytes 3145728 | tf_op jit(solution)/shard_map/all_to_all | solution.py:11
  62.4 6.1 %pad.105 = f32[31,96,96]{1,2,0:T(8,128)} pad(f32[16,96,96]{1,2,0:T(8,128)S(1)} %pad_maximum_fusion, f32[]{:T(128)} %constant.5.clone.1), padding=0_0_1x0_0_0x0_0_0 | pad | bytes 1732612 | tf_op jit(solution)/shard_map/slice | solution.py:93
  68.5 0.2 pad.107
  69.0 3.2 %slice_add_fusion.3 = f32[31,96,96]{1,2,0:T(8,128)} fusion(f32[31,96,96]{1,2,0:T(8,128)} %pad.105, f32[32,96,96]{1,2,0:T(8,128)} %pad.72), kind=kLoop, calls=%fused_computation.114 | loop fusion | flops 285696 | bytes 3428352 | tf_op jit(solution)/shard_map/add | solution.py:84
  72.1 29.6 %all-to-all-done = f32[32,97,96]{1,2,0:T(8,128)S(1)} async-done(((f32[32,97,96]{1,2,0:T(8,128)}), f32[32,97,96]{1,2,0:T(8,128)S(1)}, u32[]{:S(2)}, u32[]{:S(2)}) %all-to-all-start) | async-done | bytes 1191968 | tf_op jit(solution)/shard_map/all_to_all | solution.py:11
  101.7 0.6 broadcast_in_dim.38
  102.3 5.8 %all-to-all-start.1 = ((f32[32,96,2]{1,2,0:T(2,128)}), f32[32,96,2]{1,2,0:T(2,128)S(1)}, u32[]{:S(2)}, u32[]{:S(2)}) async-start(f32[32,96,2]{1,2,0:T(2,128)} %broadcast_in_dim.38), calls=%async_computation.1 | async-start | bytes 65536 | tf_op jit(solution)/shard_map/all_to_all | solution.py:11
  108.1 1.6 slice.325
  109.8 1.9 %copy.139 = f32[32,1,96]{2,0,1:T(8,128)S(1)} copy(f32[32,1,96]{1,2,0:T(8,128)} %slice.325) | data formatting | bytes 24576
  111.8 1.6 copy.138
  113.4 1.6 broadcast_select_fusion
  115.0 0.9 fusion.13
  116.0 1.3 fusion.17
  117.3 1.3 fusion.26
  118.6 0.7 fusion.30
  119.4 1.4 fusion.39
  120.7 1.3 fusion.43
  122.1 0.3 fusion.52
  122.4 0.2 fusion.56
  122.6 0.2 fusion.63
  123.0 0.3 fusion.11
  123.3 1.1 fusion.7
  124.4 2.7 %fusion.10 = f32[64,48,32]{0,1,2:T(8,128)} fusion(f32[64,96,32]{1,0,2:T(8,128)S(1)} %fusion.7, f32[32,48,96]{2,1,0:T(8,128)S(1)} %copy-done, f32[48,32]{0,1:T(8,128)S(1)} %bitcast.140), kind=kOutput, calls=%fused_computation.7 | convolution fusion | flops 113344512 | bytes 1775616 | tf_op jit(solution)/shard_map/tai,sit->sat/dot_general | solution.py:101
  127.1 2.1 %copy.90 = f32[64,48,32]{1,2,0:T(8,128)S(1)} copy(f32[64,48,32]{0,1,2:T(8,128)} %fusion.10) | data formatting | bytes 786432 | tf_op jit(solution)/shard_map/sub | solution.py:101
  129.1 1.7 reshape.124
  130.9 9.6 %all-to-all-start.3 = ((f32[32,1,3072]{2,1,0:T(1,128)}), f32[32,1,3072]{2,1,0:T(1,128)S(1)}, u32[]{:S(2)}, u32[]{:S(2)}) async-start(f32[32,1,3072]{2,1,0:T(1,128)} %reshape.124), calls=%async_computation.3 | async-start | bytes 786432 | tf_op jit(solution)/shard_map/all_to_all | solution.py:106
  140.5 1.6 copy.88
  142.1 11.8 %all-to-all-done.3 = f32[32,1,3072]{2,1,0:T(1,128)S(1)} async-done(((f32[32,1,3072]{2,1,0:T(1,128)}), f32[32,1,3072]{2,1,0:T(1,128)S(1)}, u32[]{:S(2)}, u32[]{:S(2)}) %all-to-all-start.3) | async-done | bytes 393248 | tf_op jit(solution)/shard_map/all_to_all | solution.py:106
  153.9 5.5 %all-to-all-start.2 = ((f32[64,96,32]{1,2,0:T(8,128)}), f32[64,96,32]{1,2,0:T(8,128)S(1)}, u32[]{:S(2)}, u32[]{:S(2)}) async-start(f32[64,96,32]{1,2,0:T(8,128)} %copy.88), calls=%async_computation.2 | async-start | bytes 2097152 | tf_op jit(solution)/shard_map/all_to_all | solution.py:105
  159.3 0.5 broadcast.60
  159.8 1.6 reduce.14
  161.4 1.5 reshape.125
  162.9 2.5 %copy.91 = f32[2,48,32,32]{3,2,1,0:T(8,128)S(1)} copy(f32[2,48,32,32]{1,3,0,2:T(8,128)} %bitcast.132) | data formatting | bytes 786432 | tf_op jit(solution)/shard_map/all_to_all | solution.py:106
  165.5 1.5 all_to_all.41
  166.9 19.0 %all-to-all-done.2 = f32[64,96,32]{1,2,0:T(8,128)S(1)} async-done(((f32[64,96,32]{1,2,0:T(8,128)}), f32[64,96,32]{1,2,0:T(8,128)S(1)}, u32[]{:S(2)}, u32[]{:S(2)}) %all-to-all-start.2) | async-done | bytes 786464 | tf_op jit(solution)/shard_map/all_to_all | solution.py:105
  186.0 1.2 copy.92
  (118 shorter events, 5.9 us)
Async XLA Ops:
  0.6 123.8 %copy-start = (f32[32,48,96]{2,1,0:T(8,128)S(1)}, f32[32,48,96]{2,1,0:T(8,128)}, u32[]{:S(2)}) copy-start(f32[32,48,96]{2,1,0:T(8,128)} %param.6) | copy-start | bytes 1769476
  4.3 1.3 copy-start.5
  4.6 0.7 copy-start.7
  10.5 7.7 %copy-start.1 = (f32[32,96,96]{2,1,0:T(8,128)S(1)}, f32[32,96,96]{2,1,0:T(8,128)}, u32[]{:S(2)}) copy-start(f32[32,96,96]{2,1,0:T(8,128)} %param.5) | copy-start | bytes 3538948
  17.3 0.9 copy-start.4
  20.7 9.7 %copy-start.9 = (f32[32,96]{1,0:T(8,128)S(1)}, f32[32,96]{1,0:T(8,128)}, u32[]{:S(2)}) copy-start(f32[32,96]{1,0:T(8,128)} %param.8) | copy-start | bytes 36868
  34.2 3.2 %copy-start.6 = (f32[4,96,96]{1,2,0:T(8,128)S(1)}, f32[4,96,96]{1,2,0:T(8,128)}, u32[]{:S(2)}) copy-start(f32[4,96,96]{1,2,0:T(8,128)} %copy-done.5) | copy-start | bytes 442372
  34.2 3.5 %copy-start.8 = (f32[2,96,96]{1,2,0:T(8,128)S(1)}, f32[2,96,96]{1,2,0:T(8,128)}, u32[]{:S(2)}) copy-start(f32[2,96,96]{1,2,0:T(8,128)} %copy-done.7) | copy-start | bytes 221188
  38.5 2.1 %slice-start = ((f32[32,96,96]{2,1,0:T(8,128)}), f32[1,96,96]{2,1,0:T(8,128)S(1)}, s32[]{:S(2)}) async-start(f32[32,96,96]{2,1,0:T(8,128)} %param.5), calls=%async_computation.4 | async-start | bytes 98304 | tf_op jit(solution)/shard_map/slice | solution.py:84
  41.9 6.2 %copy-start.2 = (f32[32,96,96]{2,1,0:T(8,128)S(1)}, f32[32,96,96]{2,1,0:T(8,128)}, u32[]{:S(2)}) copy-start(f32[32,96,96]{2,1,0:T(8,128)} %param.5) | copy-start | bytes 3538948
  41.9 7.5 %slice-start.1 = ((f32[32,96]{1,0:T(8,128)}), f32[1,96]{1,0:T(1,128)S(1)}, s32[]{:S(2)}) async-start(f32[32,96]{1,0:T(8,128)} %param.8), calls=%async_computation.5 | async-start | bytes 1024 | tf_op jit(solution)/shard_map/slice | solution.py:84
  52.4 49.3 %all-to-all-start = ((f32[32,97,96]{1,2,0:T(8,128)}), f32[32,97,96]{1,2,0:T(8,128)S(1)}, u32[]{:S(2)}, u32[]{:S(2)}) async-start(f32[32,97,96]{1,2,0:T(8,128)} %broadcast_in_dim.36), calls=%async_computation | async-start | bytes 3145728 | tf_op jit(solution)/shard_map/all_to_all | solution.py:11
  69.0 32.8 %copy-start.11 = (f32[96,2]{0,1:T(2,128)S(1)}, f32[96,2]{0,1:T(2,128)}, u32[]{:S(2)}) copy-start(f32[96,2]{0,1:T(2,128)} %param.9) | copy-start | bytes 2308
  102.3 20.7 %all-to-all-start.1 = ((f32[32,96,2]{1,2,0:T(2,128)}), f32[32,96,2]{1,2,0:T(2,128)S(1)}, u32[]{:S(2)}, u32[]{:S(2)}) async-start(f32[32,96,2]{1,2,0:T(2,128)} %broadcast_in_dim.38), calls=%async_computation.1 | async-start | bytes 65536 | tf_op jit(solution)/shard_map/all_to_all | solution.py:11
  117.3 6.0 %copy-start.3 = (f32[31,96,96]{1,2,0:T(8,128)S(1)}, f32[31,96,96]{1,2,0:T(8,128)}, u32[]{:S(2)}) copy-start(f32[31,96,96]{1,2,0:T(8,128)} %slice_add_fusion.3) | copy-start | bytes 3428356
  122.4 2.0 %copy-start.10 = (f32[32,48]{1,0:T(8,128)S(1)}, f32[32,48]{1,0:T(8,128)}, u32[]{:S(2)}) copy-start(f32[32,48]{1,0:T(8,128)} %param.7) | copy-start | bytes 18436
  130.9 23.0 %all-to-all-start.3 = ((f32[32,1,3072]{2,1,0:T(1,128)}), f32[32,1,3072]{2,1,0:T(1,128)S(1)}, u32[]{:S(2)}, u32[]{:S(2)}) async-start(f32[32,1,3072]{2,1,0:T(1,128)} %reshape.124), calls=%async_computation.3 | async-start | bytes 786432 | tf_op jit(solution)/shard_map/all_to_all | solution.py:106
  153.9 32.1 %all-to-all-start.2 = ((f32[64,96,32]{1,2,0:T(8,128)}), f32[64,96,32]{1,2,0:T(8,128)S(1)}, u32[]{:S(2)}, u32[]{:S(2)}) async-start(f32[64,96,32]{1,2,0:T(8,128)} %copy.88), calls=%async_computation.2 | async-start | bytes 2097152 | tf_op jit(solution)/shard_map/all_to_all | solution.py:105
where the time goes:
time: 189 us; the launch traced here: 187 us
  waiting for transfers between devices  60.4 us (32%)
  local copies, waits for them, and re-layouts  58.6 us (31%)
  starting transfers between devices  30.8 us (16%)
  matrix products  23.6 us (12%)
  other arithmetic  12.4 us (7%)
    all_to_all x2, waiting for transfers between devices, copy_for_each(): return lax.all_to_all(copies, axis, split_axis=0, concat_axis=0, tiled=True)  29.6 us
    pad x16, local copies, waits for them, and re-layouts, body(): prefix, offsets = lax.associative_scan(compose, (closed_loop, drift_terms))  26 us
    all_to_all x1, waiting for transfers between devices, body(): lax.all_to_all(states, 'tm', split_axis=0, concat_axis=2, tiled=True)  19 us
    all_to_all x2, starting transfers between devices, copy_for_each(): return lax.all_to_all(copies, axis, split_axis=0, concat_axis=0, tiled=True)  15.8 us
    all_to_all x1, waiting for transfers between devices, body(): lax.all_to_all(controls, 'tm', split_axis=0, concat_axis=2, tiled=True)  11.8 us
    all_to_all x1, starting transfers between devices, body(): lax.all_to_all(controls, 'tm', split_axis=0, concat_axis=2, tiled=True)  9.61 us
    unnamed x35, local copies, waits for them, and re-layouts  9.5 us
    dot_general x9, matrix products, compose(): jnp.einsum('tij,tjk->tik', second_matrix, first_matrix, precision=highest)  7.44 us
  transfers between devices with their start and end apart: 4, of which 3 were waited for; matrix products, arithmetic and copies ran while one was open for 17% of the time, Pallas kernels for 0%

commit v1 on v0

v1 whole, which is shorter than its diff:
```python
import functools

import jax
import jax.numpy as jnp
from jax import lax
from jax.experimental import pallas as pl
from jax.experimental.pallas import tpu as pltpu
from jax.sharding import PartitionSpec as P

f32, bf16 = jnp.float32, jnp.bfloat16
LANES = 128
LIMIT = 40 * 1024 * 1024


def split(x):
    high = x.astype(bf16)
    return high, (x - high.astype(f32)).astype(bf16)


def dot(a, b):
    return jnp.dot(a, b, preferred_element_type=f32)


def dot_t(a, b):
    return lax.dot_general(a, b, (((1,), (1,)), ((), ())), preferred_element_type=f32)


def extended(x):
    n = x.shape[0]
    high, low = split(x)
    shape = (LANES - n, LANES)
    row, lane = (lax.broadcasted_iota(jnp.int32, shape, d) for d in (0, 1))
    one = jnp.where((row == 0) & (lane >= n), 1.0, 0.0).astype(bf16)
    return (
        jnp.concatenate([high, one], axis=0),
        jnp.concatenate([low, jnp.zeros(shape, bf16)], axis=0),
    )


def compose(later, earlier):
    lh, ll = split(later)
    eh, el = extended(earlier)
    return dot(lh, eh) + (dot(lh, el) + dot(ll, eh))


def carry(rows, following):
    rh, rl = split(rows)
    mh, ml = extended(following)
    return dot_t(rh, mh) + (dot_t(rh, ml) + dot_t(rl, mh))


def with_offset(matrix, offset):
    wide = jnp.broadcast_to(offset, (matrix.shape[0], LANES - matrix.shape[1]))
    return jnp.concatenate([matrix, wide], axis=1)


def rounds(read, levels, count):
    get = read
    for level in levels:
        count //= 2
        for k in range(count):
            level[k] = compose(get(2 * k + 1), get(2 * k))
        get = lambda k, level=level: level[k]
    return compose(get(1), get(0))


def summary_kernel(a_ref, d_ref, x_ref, out_ref, *rest):
    maps, levels = rest[0], rest[1:]
    steps, n = d_ref.shape
    offsets = jnp.transpose(d_ref[...])
    for t in range(steps):
        maps[t] = with_offset(a_ref[t], offsets[:, t : t + 1])
    total = rounds(lambda t: maps[t], levels, steps)
    tail = jnp.pad(x_ref[...], ((0, 6), (0, LANES - n)))
    for j in range(out_ref.shape[0]):
        out_ref[j, :n] = total
        out_ref[j, n:] = tail


def prefix_kernel(k_ref, f_ref, maps, l1, l2, l3, l4, high_ref, low_ref, rows_ref):
    steps, m, n = k_ref.shape
    feeds = jnp.transpose(f_ref[...])
    row, lane = (lax.broadcasted_iota(jnp.int32, (n, LANES), d) for d in (0, 1))
    unit = jnp.where(row == lane, 1.0, 0.0).astype(f32)
    levels = (maps, l1, l2, l3, l4)

    def put(t, value):
        rows_ref[pl.ds(t, n, stride=steps)] = value

    def get(t):
        return rows_ref[pl.ds(t, n, stride=steps)]

    put(0, unit)
    for depth in range(4, -1, -1):
        size = 1 << depth
        put(size, levels[depth][0])
        for t in range(2 * size, steps, 2 * size):
            put(t + size, compose(levels[depth][t // size], get(t)))
    for t in range(steps):
        gain = with_offset(-k_ref[t], feeds[:, t : t + 1])
        rows_ref[pl.ds(n * steps + t, m, stride=steps)] = compose(gain, get(t))
    block = 512
    for at in range(0, (n + m) * steps, block):
        high, low = split(rows_ref[at : at + block])
        high_ref[at : at + block] = high
        low_ref[at : at + block] = low


def group_kernel(r_ref, out_ref, l1, l2, l3):
    count, rows, _ = r_ref.shape
    n = rows - 8
    out_ref[:n] = rounds(lambda j: r_ref[j, :n], (l1, l2, l3), count)
    for s in range(2):
        for j in range(count):
            out_ref[n + s * count + j : n + s * count + j + 1] = r_ref[j, n + s : n + s + 1]


def inner_kernel(i_ref, r_ref, l1, l2, l3, out_ref):
    n = out_ref.shape[0]
    index = i_ref[0]
    row, lane = (lax.broadcasted_iota(jnp.int32, (n, LANES), d) for d in (0, 1))
    held = jnp.where(row == lane, 1.0, 0.0).astype(f32)
    held = jnp.where((index & 8) != 0, l3[0], held)
    for bit, read in (
        (4, lambda k: l2[k]),
        (2, lambda k: l1[k]),
        (1, lambda k: r_ref[k, :n]),
    ):
        at = (index // (2 * bit)) * 2
        held = jnp.where((index & bit) != 0, compose(read(at), held), held)
    out_ref[...] = held


def apply_kernel(i_ref, own_ref, other_ref, inner_ref, high_ref, low_ref, out_ref):
    n = inner_ref.shape[0]
    second = i_ref[0] >= 16
    own, other = own_ref[n:], other_ref[n:]
    halves = jnp.where(second, other, own), jnp.where(second, own, other)
    start = jnp.concatenate([h[16 * s : 16 * s + 16] for s in (0, 1) for h in halves], axis=0)
    lane = lax.broadcasted_iota(jnp.int32, start.shape, 1)
    start = jnp.where(lane < n, start, jnp.where(lane == n, 1.0, 0.0))
    start = jnp.where(second, carry(start, other_ref[:n]), start)
    xh, xl = split(carry(start, inner_ref[...]))
    count = high_ref.shape[0] // LANES
    first = count * 2 // 3
    rest = count - first
    for q in range(count):
        at = slice(q * LANES, (q + 1) * LANES)
        high = high_ref[at]
        value = dot_t(xh, high) + (dot_t(xl, high) + dot_t(xh, low_ref[at]))
        for s in (0, 1):
            line = s * first + q if q < first else 2 * first + s * rest + q - first
            out_ref[pl.ds(line, 32, stride=2 * count)] = value[32 * s : 32 * s + 32]


def order_kernel(r_ref, states_ref, controls_ref, tile_ref):
    lines = r_ref.shape[1]
    lane = lax.broadcasted_iota(jnp.int32, (lines, LANES), 1) // 32
    cut = states_ref.shape[0]
    for g in range(8):
        parts = [r_ref[4 * g + b] for b in range(4)]
        across = slice(g * LANES, (g + 1) * LANES)
        for a in range(4):
            value = None
            for b in range(4):
                moved = parts[b] if a == b else pltpu.roll(parts[b], 32 * ((b - a) % 4), 1)
                value = moved if value is None else jnp.where(lane == b, moved, value)
            tile_ref[pl.ds(g * 4 * lines + a, lines, stride=4)] = value
        base = g * 4 * lines
        states_ref[:, across] = tile_ref[base : base + cut]
        controls_ref[:, across] = tile_ref[base + cut : base + 4 * lines]


def call(kernel, outs, scratch=(), scalars=0, inputs=0, flops=0):
    vmem = pl.BlockSpec(memory_space=pltpu.VMEM)
    smem = pl.BlockSpec(memory_space=pltpu.SMEM)
    many = isinstance(outs, (list, tuple))
    return pl.pallas_call(
        kernel,
        out_shape=outs,
        in_specs=[smem] * scalars + [vmem] * inputs,
        out_specs=[vmem] * len(outs) if many else vmem,
        scratch_shapes=list(scratch),
        compiler_params=pltpu.CompilerParams(vmem_limit_bytes=LIMIT),
        cost_estimate=pl.CostEstimate(flops=flops, bytes_accessed=4000000, transcendentals=0),
    )


def body(closed_loop, gains, feedforward, drift_terms, initial_states):
    steps, n, _ = closed_loop.shape
    m = gains.shape[1]
    blocks = lax.axis_size("tm")
    half = blocks // 2
    shape = jax.ShapeDtypeStruct
    index = lax.axis_index("tm").astype(jnp.int32)
    inner_index = (index % half).reshape(1)
    index = index.reshape(1)

    def maps_of(count):
        return shape((count, n, LANES), f32)

    payload, *levels = call(
        summary_kernel,
        [shape((half, n + 8, LANES), f32)] + [maps_of(steps >> k) for k in range(5)],
        inputs=3,
        flops=300_000_000,
    )(closed_loop, drift_terms, jnp.transpose(initial_states))
    groups = [[h * half + j for j in range(half)] for h in range(2)]
    gathered = lax.all_to_all(payload, "tm", 0, 0, tiled=True, axis_index_groups=groups)

    high, low = call(
        prefix_kernel,
        [shape(((n + m) * steps, LANES), bf16)] * 2,
        scratch=[pltpu.VMEM(((n + m) * steps, LANES), f32)],
        inputs=7,
        flops=500_000_000,
    )(gains, feedforward, *levels)

    own, *group_levels = call(
        group_kernel,
        [shape((n + 2 * half, LANES), f32)] + [maps_of(half >> k) for k in (1, 2, 3)],
        inputs=1,
        flops=150_000_000,
    )(gathered)
    other = lax.ppermute(own, "tm", [(j, (j + half) % blocks) for j in range(blocks)])
    inner = call(
        inner_kernel, shape((n, LANES), f32), scalars=1, inputs=4, flops=50_000_000
    )(inner_index, gathered, *group_levels)

    lines = 2 * (n + m) * steps // LANES
    sent = call(
        apply_kernel,
        shape((blocks * lines, LANES), f32),
        scalars=1,
        inputs=5,
        flops=300_000_000,
    )(index, own, other, inner, high, low)
    moved = lax.all_to_all(sent.reshape(blocks, lines, LANES), "tm", 0, 0, tiled=True)
    states, controls = call(
        order_kernel,
        [shape((2 * n, blocks * steps), f32), shape((2 * m, blocks * steps), f32)],
        scratch=[pltpu.VMEM((8 * 4 * lines, LANES), f32)],
        inputs=1,
        flops=1_000_000,
    )(moved)
    return states.reshape(2, n, -1), controls.reshape(2, m, -1)


def solution(mesh):
    return jax.shard_map(
        body,
        mesh=mesh,
        in_specs=(
            P("tm", None, None),
            P("tm", None, None),
            P("tm", None),
            P("tm", None),
            P(None, ("tm", "scen")),
        ),
        out_specs=(P(("tm", "scen"), None, None), P(("tm", "scen"), None, None)),
        check_vma=False,
    )
```

time: 189 us -> 94.6 us (0.50)
  blocking collectives: 0 us -> 67.6 us
  waiting for transfers between devices: 60.4 us -> 0.01 us
  local copies, waits for them, and re-layouts: 58.6 us -> 7.51 us
  starting transfers between devices: 30.8 us -> 4.63 us
  matrix products: 23.6 us -> 0 us
  Pallas kernels: 0 us -> 13.5 us
  other arithmetic: 12.4 us -> 0 us
    all_to_all x0 -> x2, blocking collectives: none -> 67.6 us  [the longest x1 36.9 us: body(): lax.all_to_all(sent.reshape(blocks, lines, LANES), 'tm', 0, 0, tiled=True)]
    all_to_all x4 -> x0, waiting for transfers between devices: 60.4 us -> none  [the longest x2 29.6 us: copy_for_each(): return lax.all_to_all(copies, axis, split_axis=0, concat_axis=0, tiled=True)]
    all_to_all x4 -> x0, starting transfers between devices: 30.8 us -> none  [the longest x2 15.8 us: copy_for_each(): return lax.all_to_all(copies, axis, split_axis=0, concat_axis=0, tiled=True)]
    pad x16 -> x0, local copies, waits for them, and re-layouts: 26 us -> none  [body(): prefix, offsets = lax.associative_scan(compose, (closed_loop, drift_terms))]
    dot_general x26 -> x0, matrix products: 23.6 us -> none  [the longest x9 7.44 us: compose(): jnp.einsum('tij,tjk->tik', second_matrix, first_matrix, precision=highest)]
    pallas_call x0 -> x6, Pallas kernels: none -> 13.5 us  [the longest x1 4.36 us: body(): call(prefix_kernel, [shape(((n + m) * steps, LANES), bf16)] * 2, scratch=...]
    slice x33 -> x0, local copies, waits for them, and re-layouts: 11.4 us -> none  [the longest x1 6.1 us: body(): lead_maps = jnp.concatenate([identity_map[None], prefix[:-1]], axis=0)]
    add x24 -> x0, other arithmetic: 5.74 us -> none  [the longest x13 5.67 us: body(): prefix, offsets = lax.associative_scan(compose, (closed_loop, drift_terms))]
  transfers between devices with their start and end apart: 4 -> 1, of which waited for: 3 -> 0; matrix products, arithmetic and copies ran while one was open for 17% -> 0% of each run, Pallas kernels for 0% -> 5%
where the time goes in v1:
time: 94.6 us; the launch traced here: 94.1 us
  blocking collectives  67.6 us (71%)
  Pallas kernels  13.5 us (14%)
  local copies, waits for them, and re-layouts  7.51 us (8%)
  starting transfers between devices  4.63 us (5%)
    all_to_all x1, blocking collectives, body(): lax.all_to_all(sent.reshape(blocks, lines, LANES), 'tm', 0, 0, tiled=True)  36.9 us
    all_to_all x1, blocking collectives, body(): lax.all_to_all(payload, 'tm', 0, 0, tiled=True, axis_index_groups=groups)  30.7 us
    unnamed x30, local copies, waits for them, and re-layouts  7.51 us
    ppermute x1, starting transfers between devices, body(): lax.ppermute(own, 'tm', [(j, (j + half) % blocks) for j in range(blocks)])  4.63 us
    pallas_call x1, Pallas kernels, body(): call(prefix_kernel, [shape(((n + m) * steps, LANES), bf16)] * 2, scratch=...  4.36 us
    pallas_call x1, Pallas kernels, body(): call(apply_kernel, shape((blocks * lines, LANES), f32), scalars=1, inputs...  3.65 us
    pallas_call x1, Pallas kernels, body(): call(order_kernel, [shape((2 * n, blocks * steps), f32), shape((2 * m, bl...  2.08 us
  transfers between devices with their start and end apart: 1, of which 0 were waited for; matrix products, arithmetic and copies ran while one was open for 0% of the time, Pallas kernels for 5%

profile of v1, /device:TPU:448, one launch (start us, length us, event | category | flops | bytes accessed | tf_op | source)
XLA Modules:
  0.0 94.1 jit_solution(8416508948762080918)
XLA Ops:
  0.6 0.0 copy-start
  0.6 1.4 %copy-done = f32[32,96,96]{2,1,0:T(8,128)S(1)} copy-done((f32[32,96,96]{2,1,0:T(8,128)S(1)}, f32[32,96,96]{2,1,0:T(8,128)}, u32[]{:S(2)}) %copy-start) | copy-done | bytes 1179672
  2.0 0.0 copy-start.12
  2.0 0.7 copy-done.12
  2.8 0.0 copy-start.14
  2.8 0.7 copy-done.14
  3.4 1.6 %shard_map.68 = (f32[16,104,128]{2,1,0:T(8,128)S(1)}, f32[32,96,128]{2,1,0:T(8,128)S(1)}, f32[16,96,128]{2,1,0:T(8,128)S(1)}, f32[8,96,128]{2,1,0:T(8,128)S(1)},...) custom-call(f32[32,96,96]{2,1,0:T(8,128)S(1)} %copy-done, f32[32,96]{1,0:T(8,128)S(1)} %copy-done.12, ...), custom_call_target="tpu_custom_call" | custom-call | flops 300000000 | bytes 4000000 | tf_op jit(solution)/shard_map/pallas_call | solution.py:202
  5.0 0.0 copy-start.2
  5.0 0.0 copy-start.4
  5.0 0.0 copy-start.8
  5.1 0.0 copy-start.10
  5.1 0.0 copy-start.1
  5.1 0.0 copy-start.13
  5.1 30.7 %all_to_all.10.r_ref = f32[16,104,128]{2,1,0:T(8,128)S(1)} all-to-all(f32[16,104,128]{2,1,0:T(8,128)S(1)} %get-tuple-element.16), channel_id=1, replica_groups={{0,16,32,48,64,80,96,112,128,144,160,176,192,208,224,240},{256,272,288,..., dimensions={0} | all-to-all | bytes 1703936 | tf_op jit(solution)/shard_map/all_to_all | solution.py:209
  35.7 1.4 %shard_map.69 = (f32[128,128]{1,0:T(8,128)}, f32[8,96,128]{2,1,0:T(8,128)S(1)}, f32[4,96,128]{2,1,0:T(8,128)S(1)}, f32[2,96,128]{2,1,0:T(8,128)S(1)}) custom-call(f32[16,104,128]{2,1,0:T(8,128)S(1)} %all_to_all.10.r_ref), custom_call_target="tpu_custom_call" | custom-call | flops 150000000 | bytes 4000000 | tf_op jit(solution)/shard_map/pallas_call | solution.py:219
  37.1 0.0 copy-done.2
  37.1 0.0 copy-done.4
  37.1 0.0 copy-done.8
  37.1 0.0 copy-done.10
  37.1 0.0 copy-start.6
  37.2 0.7 copy-done.6
  37.9 4.6 %collective-permute-start = (f32[128,128]{1,0:T(8,128)}, f32[128,128]{1,0:T(8,128)}, u32[]{:S(2)}, u32[]{:S(2)}) collective-permute-start(f32[128,128]{1,0:T(8,128)} %get-tuple-element.17.own_ref), channel_id=1, source_target_pairs={{0,256},{16,272},{32,288},{48,304},{64,320},{80,336},{96,352},{112... | collective-permute-start | bytes 196616 | tf_op jit(solution)/shard_map/ppermute | solution.py:225
  42.6 0.0 copy-done.1
  42.6 0.0 copy-done.13
  42.6 0.0 copy-start.3
  42.6 1.1 %copy-done.3 = f32[16,96,128]{2,1,0:T(8,128)S(1)} copy-done((f32[16,96,128]{2,1,0:T(8,128)S(1)}, f32[16,96,128]{2,1,0:T(8,128)}, u32[]{:S(2)}) %copy-start.3) | copy-done | bytes 786456
  43.7 0.0 copy-start.5
  43.7 1.0 %copy-done.5 = f32[8,96,128]{2,1,0:T(8,128)S(1)} copy-done((f32[8,96,128]{2,1,0:T(8,128)S(1)}, f32[8,96,128]{2,1,0:T(8,128)}, u32[]{:S(2)}) %copy-start.5) | copy-done | bytes 393240
  44.7 0.0 copy-start.9
  44.7 0.9 copy-done.9
  45.6 0.0 copy-start.11
  45.6 0.9 copy-done.11
  46.5 0.0 copy-start.7
  46.5 4.4 %shard_map.71 = (bf16[4608,128]{1,0:T(8,128)(2,1)S(1)}, bf16[4608,128]{1,0:T(8,128)(2,1)S(1)}) custom-call(f32[32,48,96]{2,1,0:T(8,128)S(1)} %copy-done.1, f32[32,48]{1,0:T(8,128)S(1)} %copy-done.13, f32[32,96,128]{2,1,0:T(8,128)S(1)} %get-tuple-element.21.maps, f32[16,96,128]{2,1,0:T(8,128)S(1)} %copy-done.3, f32[8,96,128]{2,1,0:T(8,128)S(1)} %copy-done.5, ...), custom_call_target="tpu_custom_call" | custom-call | flops 500000000 | bytes 4000000 | tf_op jit(solution)/shard_map/pallas_call | solution.py:211
  50.9 0.0 copy-done.7
  50.9 0.5 shard_map.70.inner_ref
  51.4 0.0 collective-permute-done.other_ref
  51.4 3.6 %shard_map.72 = f32[2304,128]{1,0:T(8,128)S(1)} custom-call(s32[1]{0:T(128)} %bitcast.i_ref, f32[128,128]{1,0:T(8,128)} %get-tuple-element.17.own_ref, f32[128,128]{1,0:T(8,128)} %collective-permute-done.other_ref, f32[96,128]{1,0:T(8,128)S(1)} %shard_map.70.inner_ref, bf16[4608,128]{1,0:T(8,128)(2,1)S(1)} %get-tuple-element.26.high_ref, ...), custom_call_target="tpu_custom_call" | custom-call | flops 300000000 | bytes 4000000 | tf_op jit(solution)/shard_map/pallas_call | solution.py:231
  55.1 36.9 %all_to_all.11.r_ref = f32[32,72,128]{2,1,0:T(8,128)S(1)} all-to-all(f32[32,72,128]{2,1,0:T(8,128)S(1)} %bitcast.6), channel_id=1, replica_groups=mesh['tm'=32,'scen'=16] {'tm'}, dimensions={0} | all-to-all | bytes 2359296 | tf_op jit(solution)/shard_map/all_to_all | solution.py:238
  92.0 2.1 %shard_map.73 = (f32[192,1024]{1,0:T(8,128)}, f32[96,1024]{1,0:T(8,128)}) custom-call(f32[32,72,128]{2,1,0:T(8,128)S(1)} %all_to_all.11.r_ref), custom_call_target="tpu_custom_call" | custom-call | flops 1000000 | bytes 4000000 | tf_op jit(solution)/shard_map/pallas_call | solution.py:239
Async XLA Ops:
  0.6 1.4 %copy-start = (f32[32,96,96]{2,1,0:T(8,128)S(1)}, f32[32,96,96]{2,1,0:T(8,128)}, u32[]{:S(2)}) copy-start(f32[32,96,96]{2,1,0:T(8,128)} %a_ref.1) | copy-start | bytes 3538948
  2.0 0.7 copy-start.12
  2.8 0.7 copy-start.14
  5.0 32.1 %copy-start.2 = (f32[16,96,128]{2,1,0:T(8,128)}, f32[16,96,128]{2,1,0:T(8,128)S(1)}, u32[]{:S(2)}) copy-start(f32[16,96,128]{2,1,0:T(8,128)S(1)} %get-tuple-element.22.l1) | copy-start | bytes 2359300
  5.0 32.1 %copy-start.4 = (f32[8,96,128]{2,1,0:T(8,128)}, f32[8,96,128]{2,1,0:T(8,128)S(1)}, u32[]{:S(2)}) copy-start(f32[8,96,128]{2,1,0:T(8,128)S(1)} %get-tuple-element.23.l2) | copy-start | bytes 1179652
  5.0 32.1 %copy-start.8 = (f32[4,96,128]{2,1,0:T(8,128)}, f32[4,96,128]{2,1,0:T(8,128)S(1)}, u32[]{:S(2)}) copy-start(f32[4,96,128]{2,1,0:T(8,128)S(1)} %get-tuple-element.24.l3) | copy-start | bytes 589828
  5.1 32.1 %copy-start.10 = (f32[2,96,128]{2,1,0:T(8,128)}, f32[2,96,128]{2,1,0:T(8,128)S(1)}, u32[]{:S(2)}) copy-start(f32[2,96,128]{2,1,0:T(8,128)S(1)} %get-tuple-element.25.l4) | copy-start | bytes 294916
  5.1 37.5 %copy-start.1 = (f32[32,48,96]{2,1,0:T(8,128)S(1)}, f32[32,48,96]{2,1,0:T(8,128)}, u32[]{:S(2)}) copy-start(f32[32,48,96]{2,1,0:T(8,128)} %k_ref.1) | copy-start | bytes 1769476
  5.1 37.5 %copy-start.13 = (f32[32,48]{1,0:T(8,128)S(1)}, f32[32,48]{1,0:T(8,128)}, u32[]{:S(2)}) copy-start(f32[32,48]{1,0:T(8,128)} %f_ref.1) | copy-start | bytes 18436
  37.1 0.7 copy-start.6
  37.9 13.5 %collective-permute-start = (f32[128,128]{1,0:T(8,128)}, f32[128,128]{1,0:T(8,128)}, u32[]{:S(2)}, u32[]{:S(2)}) collective-permute-start(f32[128,128]{1,0:T(8,128)} %get-tuple-element.17.own_ref), channel_id=1, source_target_pairs={{0,256},{16,272},{32,288},{48,304},{64,320},{80,336},{96,352},{112... | collective-permute-start | bytes 196616 | tf_op jit(solution)/shard_map/ppermute | solution.py:225
  42.6 1.1 %copy-start.3 = (f32[16,96,128]{2,1,0:T(8,128)S(1)}, f32[16,96,128]{2,1,0:T(8,128)}, u32[]{:S(2)}) copy-start(f32[16,96,128]{2,1,0:T(8,128)} %copy-done.2) | copy-start | bytes 2359300
  43.7 1.0 %copy-start.5 = (f32[8,96,128]{2,1,0:T(8,128)S(1)}, f32[8,96,128]{2,1,0:T(8,128)}, u32[]{:S(2)}) copy-start(f32[8,96,128]{2,1,0:T(8,128)} %copy-done.4) | copy-start | bytes 1179652
  44.7 0.9 copy-start.9
  45.6 0.9 copy-start.11
  46.5 4.4 %copy-start.7 = (f32[8,96,128]{2,1,0:T(8,128)S(1)}, f32[8,96,128]{2,1,0:T(8,128)}, u32[]{:S(2)}) copy-start(f32[8,96,128]{2,1,0:T(8,128)} %copy-done.6) | copy-start | bytes 1179652

commit v2 on v1

v2 whole, which is shorter than its diff:
```python
import jax
import jax.numpy as jnp
from jax import lax
from jax.experimental import pallas as pl
from jax.experimental.pallas import tpu as pltpu
from jax.sharding import PartitionSpec as P

f32, bf16 = jnp.float32, jnp.bfloat16
LANES = 128
LIMIT = 40 * 1024 * 1024


def split(x):
    high = x.astype(bf16)
    return high, (x - high.astype(f32)).astype(bf16)


def dot(a, b):
    return jnp.dot(a, b, preferred_element_type=f32)


def dot_t(a, b):
    return lax.dot_general(a, b, (((1,), (1,)), ((), ())), preferred_element_type=f32)


def extended(x):
    n = x.shape[0]
    high, low = split(x)
    shape = (LANES - n, LANES)
    row, lane = (lax.broadcasted_iota(jnp.int32, shape, d) for d in (0, 1))
    one = jnp.where((row == 0) & (lane >= n), 1.0, 0.0).astype(bf16)
    return (
        jnp.concatenate([high, one], axis=0),
        jnp.concatenate([low, jnp.zeros(shape, bf16)], axis=0),
    )


def compose(later, earlier):
    lh, ll = split(later)
    eh, el = extended(earlier)
    return dot(lh, eh) + (dot(lh, el) + dot(ll, eh))


def carry(rows, following):
    rh, rl = split(rows)
    mh, ml = extended(following)
    return dot_t(rh, mh) + (dot_t(rh, ml) + dot_t(rl, mh))


def with_offset(matrix, offset):
    wide = jnp.broadcast_to(offset, (matrix.shape[0], LANES - matrix.shape[1]))
    return jnp.concatenate([matrix, wide], axis=1)


def rounds(maps, count, at=0):
    while count > 2:
        end = at + count
        for k in range(count // 2):
            maps[end + k] = compose(maps[at + 2 * k + 1], maps[at + 2 * k])
        at, count = end, count // 2
    return compose(maps[at + 1], maps[at])


def lanes_of(shape):
    return lax.broadcasted_iota(jnp.int32, shape, 1)


def packed(total, rows):
    n = total.shape[0]
    body, spare = 3 * n // 4, n // 4
    bottom = total[body:]
    side = jnp.concatenate(
        [pltpu.roll(bottom, (n - 32 * c) % LANES, 1) if 32 * c != n else bottom for c in range(3)],
        axis=0,
    )
    top = jnp.where(lanes_of(side.shape) < n, total[:body], side)
    offset = jnp.transpose(total)[n : n + 1]
    tail = jnp.concatenate([offset, rows, jnp.zeros((7 - rows.shape[0], n), f32)], axis=0)
    return top, jnp.pad(tail, ((0, 0), (0, LANES - n)))


def unpacked(lines, offset):
    body = lines.shape[0]
    spare = body // 3
    n = body + spare
    offset = jnp.broadcast_to(offset, (n, LANES))
    lane = lanes_of((spare, LANES))
    bottom = offset[body:]
    for c in range(3):
        part = pltpu.roll(lines[spare * c : spare * (c + 1)], (32 * c - n) % LANES, 1)
        bottom = jnp.where(lane // 32 == c, part, bottom)
    top = jnp.where(lanes_of(lines.shape) < n, lines, offset[:body])
    return jnp.concatenate([top, bottom], axis=0)


def summary_kernel(a_hbm, d_hbm, x_hbm, out_ref, maps, a_ref, d_ref, x_ref, sems):
    steps, n = d_ref.shape
    parts = 4
    size = steps // parts
    copies = [
        pltpu.make_async_copy(d_hbm, d_ref, sems.at[parts]),
        pltpu.make_async_copy(x_hbm, x_ref, sems.at[parts + 1]),
    ]
    blocks = []
    for c in range(parts):
        part = pl.ds(c * size, size)
        blocks.append(pltpu.make_async_copy(a_hbm.at[part], a_ref.at[part], sems.at[c]))
    for copy in copies[:1] + blocks + copies[1:]:
        copy.start()
    copies[0].wait()
    offsets = jnp.transpose(d_ref[...])
    for c in range(parts):
        blocks[c].wait()
        for t in range(c * size, (c + 1) * size):
            maps[t] = with_offset(a_ref[t], offsets[:, t : t + 1])
    total = rounds(maps, steps)
    copies[1].wait()
    top, tail = packed(total, x_ref[...])
    for j in range(out_ref.shape[0]):
        out_ref[j, : top.shape[0]] = top
        out_ref[j, top.shape[0] :] = tail


def prefix_kernel(k_ref, f_ref, maps, out_ref, rows_ref):
    steps, m, n = k_ref.shape
    feeds = jnp.transpose(f_ref[...])
    row, lane = (lax.broadcasted_iota(jnp.int32, (n, LANES), d) for d in (0, 1))
    unit = jnp.where(row == lane, 1.0, 0.0).astype(f32)

    def put(t, value):
        rows_ref[pl.ds(t, n, stride=steps)] = value

    def get(t):
        return rows_ref[pl.ds(t, n, stride=steps)]

    put(0, unit)
    size = steps
    while size > 1:
        size //= 2
        at = 2 * steps - 2 * (steps // size)
        put(size, maps[at])
        for t in range(2 * size, steps, 2 * size):
            put(t + size, compose(maps[at + t // size], get(t)))
    for t in range(steps):
        gain = with_offset(-k_ref[t], feeds[:, t : t + 1])
        rows_ref[pl.ds(n * steps + t, m, stride=steps)] = compose(gain, get(t))
    block = 512
    for at in range(0, (n + m) * steps, block):
        high, low = split(rows_ref[at : at + block])
        out_ref[at : at + block, :LANES] = high
        out_ref[at : at + block, LANES:] = low


def group_kernel(r_ref, out_ref, maps):
    count, lines, _ = r_ref.shape
    n = maps.shape[1]
    body = lines - 8
    heads = [
        jnp.concatenate([r_ref[j, body + k : body + k + 1] for j in range(count)], axis=0)
        for k in range(3)
    ]
    offsets = jnp.transpose(heads[0])[:n]
    for j in range(count):
        maps[j] = unpacked(r_ref[j, :body], offsets[:, j : j + 1])
    out_ref[:n] = rounds(maps, count)
    for s in range(2):
        out_ref[n + s * count : n + (s + 1) * count] = heads[1 + s]


def inner_kernel(i_ref, maps, out_ref):
    n = out_ref.shape[0]
    index = i_ref[0]
    row, lane = (lax.broadcasted_iota(jnp.int32, (n, LANES), d) for d in (0, 1))
    held = jnp.where(row == lane, 1.0, 0.0).astype(f32)
    held = jnp.where((index & 8) != 0, maps[28], held)
    for bit, first in ((4, 24), (2, 16), (1, 0)):
        at = first + (index // (2 * bit)) * 2
        held = jnp.where((index & bit) != 0, compose(maps[at], held), held)
    out_ref[...] = held


def apply_kernel(i_ref, own_ref, other_ref, inner_ref, maps_ref, out_ref):
    n = inner_ref.shape[0]
    second = i_ref[0] >= 16
    own, other = own_ref[n:], other_ref[n:]
    halves = jnp.where(second, other, own), jnp.where(second, own, other)
    start = jnp.concatenate([h[16 * s : 16 * s + 16] for s in (0, 1) for h in halves], axis=0)
    lane = lanes_of(start.shape)
    start = jnp.where(lane < n, start, jnp.where(lane == n, 1.0, 0.0))
    start = jnp.where(second, carry(start, other_ref[:n]), start)
    xh, xl = split(carry(start, inner_ref[...]))
    x = jnp.concatenate(
        [jnp.concatenate([xh, xh], axis=1), jnp.concatenate([xl, jnp.zeros_like(xl)], axis=1)],
        axis=0,
    )
    count = maps_ref.shape[0] // LANES
    first = count * 2 // 3
    rest = count - first
    for q in range(0, count, 2):
        value = dot_t(x, maps_ref[q * LANES : (q + 2) * LANES])
        value = value[:64] + value[64:]
        for p in (0, 1):
            for s in (0, 1):
                line = s * first + q + p if q < first else 2 * first + s * rest + q + p - first
                part = value[32 * s : 32 * s + 32, p * LANES : (p + 1) * LANES]
                out_ref[pl.ds(line, 32, stride=2 * count)] = part


def order_kernel(r_ref, states_hbm, controls_hbm, tile_ref, sems):
    lines = r_ref.shape[1]
    lane = lanes_of((lines, LANES)) // 32
    cut = states_hbm.shape[0]
    copies = []
    for g in range(8):
        parts = [r_ref[4 * g + b] for b in range(4)]
        for a in range(4):
            value = None
            for b in range(4):
                moved = parts[b] if a == b else pltpu.roll(parts[b], 32 * ((b - a) % 4), 1)
                value = moved if value is None else jnp.where(lane == b, moved, value)
            tile_ref[g, pl.ds(a, lines, stride=4)] = value
        across = pl.ds(g * LANES, LANES)
        for k, (rows, to) in enumerate(
            ((pl.ds(0, cut), states_hbm), (pl.ds(cut, 4 * lines - cut), controls_hbm))
        ):
            copies.append(
                pltpu.make_async_copy(tile_ref.at[g, rows], to.at[:, across], sems.at[2 * g + k])
            )
            copies[-1].start()
    for copy in copies:
        copy.wait()


VMEM = pl.BlockSpec(memory_space=pltpu.VMEM)
SMEM = pl.BlockSpec(memory_space=pltpu.SMEM)
HBM = pl.BlockSpec(memory_space=pltpu.HBM)


def call(kernel, outs, ins, to=VMEM, scratch=(), flops=0, limit=LIMIT):
    many = isinstance(outs, (list, tuple))
    return pl.pallas_call(
        kernel,
        out_shape=outs,
        in_specs=ins,
        out_specs=[to] * len(outs) if many else to,
        scratch_shapes=list(scratch),
        compiler_params=pltpu.CompilerParams(vmem_limit_bytes=limit),
        cost_estimate=pl.CostEstimate(flops=flops, bytes_accessed=4000000, transcendentals=0),
    )


def body(closed_loop, gains, feedforward, drift_terms, initial_states):
    steps, n, _ = closed_loop.shape
    m = gains.shape[1]
    blocks = lax.axis_size("tm")
    half = blocks // 2
    shape = jax.ShapeDtypeStruct
    index = lax.axis_index("tm").astype(jnp.int32)
    inner_index = (index % half).reshape(1)
    index = index.reshape(1)
    semaphores = pltpu.SemaphoreType.DMA

    payload, maps = call(
        summary_kernel,
        [shape((half, 3 * n // 4 + 8, LANES), f32), shape((2 * steps - 2, n, LANES), f32)],
        [HBM] * 3,
        scratch=[
            pltpu.VMEM((steps, n, n), f32),
            pltpu.VMEM((steps, n), f32),
            pltpu.VMEM((2, n), f32),
            semaphores((6,)),
        ],
        flops=300_000_000,
        limit=60 * 1024 * 1024,
    )(closed_loop, drift_terms, jnp.transpose(initial_states))
    groups = [[h * half + j for j in range(half)] for h in range(2)]
    gathered = lax.all_to_all(payload, "tm", 0, 0, tiled=True, axis_index_groups=groups)

    rows = (n + m) * steps
    local = call(
        prefix_kernel,
        shape((rows, 2 * LANES), bf16),
        [VMEM] * 3,
        scratch=[pltpu.VMEM((rows, LANES), f32)],
        flops=500_000_000,
    )(gains, feedforward, maps)
    gathered, local = lax.optimization_barrier((gathered, local))

    own, group_maps = call(
        group_kernel,
        [shape((n + 2 * half, LANES), f32), shape((2 * half - 2, n, LANES), f32)],
        [VMEM],
        flops=150_000_000,
    )(gathered)
    other = lax.ppermute(own, "tm", [(j, (j + half) % blocks) for j in range(blocks)])
    inner = call(inner_kernel, shape((n, LANES), f32), [SMEM, VMEM], flops=50_000_000)(
        inner_index, group_maps
    )

    lines = 2 * rows // LANES
    sent = call(
        apply_kernel,
        shape((blocks * lines, LANES), f32),
        [SMEM] + [VMEM] * 4,
        flops=300_000_000,
    )(index, own, other, inner, local)
    moved = lax.all_to_all(sent.reshape(blocks, lines, LANES), "tm", 0, 0, tiled=True)
    states, controls = call(
        order_kernel,
        [shape((2 * n, blocks * steps), f32), shape((2 * m, blocks * steps), f32)],
        [VMEM],
        to=HBM,
        scratch=[pltpu.VMEM((8, 4 * lines, LANES), f32), semaphores((16,))],
        flops=1_000_000,
    )(moved)
    return states.reshape(2, n, -1), controls.reshape(2, m, -1)


def solution(mesh):
    return jax.shard_map(
        body,
        mesh=mesh,
        in_specs=(
            P("tm", None, None),
            P("tm", None, None),
            P("tm", None),
            P("tm", None),
            P(None, ("tm", "scen")),
        ),
        out_specs=(P(("tm", "scen"), None, None), P(("tm", "scen"), None, None)),
        check_vma=False,
    )
```

time: 94.6 us -> 82.7 us (0.87)
  blocking collectives: 67.6 us -> 37.8 us
  waiting for transfers between devices: 0.01 us -> 11.8 us
  starting transfers between devices: 4.63 us -> 12.8 us
  local copies, waits for them, and re-layouts: 7.51 us -> 5.5 us
    all_to_all x1 -> x0, blocking collectives: 30.7 us -> none  [body(): lax.all_to_all(payload, 'tm', 0, 0, tiled=True, axis_index_groups=groups)]
    all_to_all x0 -> x1, waiting for transfers between devices: none -> 10.7 us  [body(): lax.all_to_all(payload, 'tm', 0, 0, tiled=True, axis_index_groups=groups)]
    all_to_all x0 -> x1, starting transfers between devices: none -> 8.14 us  [body(): lax.all_to_all(payload, 'tm', 0, 0, tiled=True, axis_index_groups=groups)]
    unnamed x30 -> x10, local copies, waits for them, and re-layouts: 7.51 us -> 5.5 us
    ppermute x1, waiting for transfers between devices: 0.01 us -> 1.13 us  [body(): lax.ppermute(own, 'tm', [(j, (j + half) % blocks) for j in range(blocks)])]
  transfers between devices with their start and end apart: 1 -> 2, of which waited for: 0 -> 2; matrix products, arithmetic and copies ran while one was open for 0% -> 0% of each run, Pallas kernels for 5% -> 6%
where the time goes in v2:
time: 82.7 us; the launch traced here: 82.4 us
  blocking collectives  37.8 us (46%)
  Pallas kernels  13.8 us (17%)
  starting transfers between devices  12.8 us (15%)
  waiting for transfers between devices  11.8 us (14%)
  local copies, waits for them, and re-layouts  5.5 us (7%)
    all_to_all x1, blocking collectives, body(): lax.all_to_all(sent.reshape(blocks, lines, LANES), 'tm', 0, 0, tiled=True)  37.8 us
    all_to_all x1, waiting for transfers between devices, body(): lax.all_to_all(payload, 'tm', 0, 0, tiled=True, axis_index_groups=groups)  10.7 us
    all_to_all x1, starting transfers between devices, body(): lax.all_to_all(payload, 'tm', 0, 0, tiled=True, axis_index_groups=groups)  8.14 us
    unnamed x10, local copies, waits for them, and re-layouts  5.5 us
    ppermute x1, starting transfers between devices, body(): lax.ppermute(own, 'tm', [(j, (j + half) % blocks) for j in range(blocks)])  4.63 us
    pallas_call x1, Pallas kernels, body(): call(summary_kernel, [shape((half, 3 * n // 4 + 8, LANES), f32), shape((2...  4.57 us
    pallas_call x1, Pallas kernels, body(): call(prefix_kernel, shape((rows, 2 * LANES), bf16), [VMEM] * 3, scratch=[...  4.52 us
    pallas_call x1, Pallas kernels, body(): call(order_kernel, [shape((2 * n, blocks * steps), f32), shape((2 * m, bl...  1.77 us
  transfers between devices with their start and end apart: 2, of which 2 were waited for; matrix products, arithmetic and copies ran while one was open for 0% of the time, Pallas kernels for 6%

profile of v2, /device:TPU:448, one launch (start us, length us, event | category | flops | bytes accessed | tf_op | source)
XLA Modules:
  0.0 82.4 jit_solution(14345342016639921903)
XLA Ops:
  0.6 0.0 copy-start.4
  0.6 4.6 %shard_map.68 = (f32[16,80,128]{2,1,0:T(8,128)}, f32[62,96,128]{2,1,0:T(8,128)}) custom-call(f32[32,96,96]{2,1,0:T(8,128)} %a_hbm.1, f32[32,96]{1,0:T(8,128)} %d_hbm.1, f32[2,96]{1,0:T(2,128)} %bitcast.7), custom_call_target="tpu_custom_call" | custom-call | flops 300000000 | bytes 4000000 | tf_op jit(solution)/shard_map/pallas_call | solution.py:263
  5.2 8.1 %all-to-all-start = ((f32[16,80,128]{2,1,0:T(8,128)}), f32[16,80,128]{2,1,0:T(8,128)S(1)}, u32[]{:S(2)}, u32[]{:S(2)}) async-start(f32[16,80,128]{2,1,0:T(8,128)} %get-tuple-element.10), calls=%async_computation | async-start | bytes 1310720 | tf_op jit(solution)/shard_map/all_to_all | solution.py:277
  13.4 0.0 copy-done.4
  13.4 0.0 copy-start
  13.4 1.9 %copy-done = f32[62,96,128]{2,1,0:T(8,128)S(1)} copy-done((f32[62,96,128]{2,1,0:T(8,128)S(1)}, f32[62,96,128]{2,1,0:T(8,128)}, u32[]{:S(2)}) %copy-start) | copy-done | bytes 3047448
  15.2 0.0 copy-start.3
  15.2 1.1 %copy-done.3 = f32[32,48,96]{2,1,0:T(8,128)S(1)} copy-done((f32[32,48,96]{2,1,0:T(8,128)S(1)}, f32[32,48,96]{2,1,0:T(8,128)}, u32[]{:S(2)}) %copy-start.3) | copy-done | bytes 589848
  16.4 4.5 %shard_map.69.maps_ref = bf16[4608,256]{1,0:T(8,128)(2,1)S(1)} custom-call(f32[32,48,96]{2,1,0:T(8,128)S(1)} %copy-done.3, f32[32,48]{1,0:T(8,128)S(1)} %copy-done.4, f32[62,96,128]{2,1,0:T(8,128)S(1)} %copy-done), custom_call_target="tpu_custom_call" | custom-call | flops 500000000 | bytes 4000000 | tf_op jit(solution)/shard_map/pallas_call | solution.py:280
  20.9 10.7 %all-to-all-done.r_ref = f32[16,80,128]{2,1,0:T(8,128)S(1)} async-done(((f32[16,80,128]{2,1,0:T(8,128)}), f32[16,80,128]{2,1,0:T(8,128)S(1)}, u32[]{:S(2)}, u32[]{:S(2)}) %all-to-all-start) | async-done | bytes 655392 | tf_op jit(solution)/shard_map/all_to_all | solution.py:277
  31.6 1.2 %shard_map.70 = (f32[128,128]{1,0:T(8,128)S(1)}, f32[30,96,128]{2,1,0:T(8,128)S(1)}) custom-call(f32[16,80,128]{2,1,0:T(8,128)S(1)} %all-to-all-done.r_ref), custom_call_target="tpu_custom_call" | custom-call | flops 150000000 | bytes 4000000 | tf_op jit(solution)/shard_map/pallas_call | solution.py:289
  32.8 0.0 copy-start.1
  32.8 1.1 %copy-done.1 = f32[30,96,128]{2,1,0:T(8,128)} copy-done((f32[30,96,128]{2,1,0:T(8,128)}, f32[30,96,128]{2,1,0:T(8,128)S(1)}, u32[]{:S(2)}) %copy-start.1) | copy-done | bytes 1474584
  33.9 4.6 %collective-permute-start = (f32[128,128]{1,0:T(8,128)S(1)}, f32[128,128]{1,0:T(8,128)S(1)}, u32[]{:S(2)}, u32[]{:S(2)}) collective-permute-start(f32[128,128]{1,0:T(8,128)S(1)} %get-tuple-element.13.own_ref), channel_id=1, source_target_pairs={{0,256},{16,272},{32,288},{48,304},{64,320},{80,336},{96,352},{112... | collective-permute-start | bytes 196616 | tf_op jit(solution)/shard_map/ppermute | solution.py:295
  38.6 0.0 copy-start.2
  38.6 1.4 %copy-done.2 = f32[30,96,128]{2,1,0:T(8,128)S(1)} copy-done((f32[30,96,128]{2,1,0:T(8,128)S(1)}, f32[30,96,128]{2,1,0:T(8,128)}, u32[]{:S(2)}) %copy-start.2) | copy-done | bytes 1474584
  40.0 0.5 shard_map.71.inner_ref
  40.5 1.1 %collective-permute-done.other_ref = f32[128,128]{1,0:T(8,128)S(1)} collective-permute-done((f32[128,128]{1,0:T(8,128)S(1)}, f32[128,128]{1,0:T(8,128)S(1)}, u32[]{:S(2)}, u32[]{:S(2)}) %collective-permute-start) | collective-permute-done | bytes 65568 | tf_op jit(solution)/shard_map/ppermute | solution.py:295
  41.6 1.2 %shard_map.72 = f32[2304,128]{1,0:T(8,128)S(1)} custom-call(s32[1]{0:T(128)} %bitcast.i_ref, f32[128,128]{1,0:T(8,128)S(1)} %get-tuple-element.13.own_ref, f32[128,128]{1,0:T(8,128)S(1)} %collective-permute-done.other_ref, f32[96,128]{1,0:T(8,128)S(1)} %shard_map.71.inner_ref, bf16[4608,256]{1,0:T(8,128)(2,1)S(1)} %shard_map.69.maps_ref), custom_call_target="tpu_custom_call" | custom-call | flops 300000000 | bytes 4000000 | tf_op jit(solution)/shard_map/pallas_call | solution.py:301
  42.8 37.8 %all_to_all.10.r_ref = f32[32,72,128]{2,1,0:T(8,128)S(1)} all-to-all(f32[32,72,128]{2,1,0:T(8,128)S(1)} %bitcast.6), channel_id=1, replica_groups=mesh['tm'=32,'scen'=16] {'tm'}, dimensions={0} | all-to-all | bytes 2359296 | tf_op jit(solution)/shard_map/all_to_all | solution.py:307
  80.6 1.8 %shard_map.73 = (f32[192,1024]{1,0:T(8,128)}, f32[96,1024]{1,0:T(8,128)}) custom-call(f32[32,72,128]{2,1,0:T(8,128)S(1)} %all_to_all.10.r_ref), custom_call_target="tpu_custom_call" | custom-call | flops 1000000 | bytes 4000000 | tf_op jit(solution)/shard_map/pallas_call | solution.py:308
Async XLA Ops:
  0.6 12.7 %copy-start.4 = (f32[32,48]{1,0:T(8,128)S(1)}, f32[32,48]{1,0:T(8,128)}, u32[]{:S(2)}) copy-start(f32[32,48]{1,0:T(8,128)} %f_ref.1) | copy-start | bytes 18436
  5.2 26.3 %all-to-all-start = ((f32[16,80,128]{2,1,0:T(8,128)}), f32[16,80,128]{2,1,0:T(8,128)S(1)}, u32[]{:S(2)}, u32[]{:S(2)}) async-start(f32[16,80,128]{2,1,0:T(8,128)} %get-tuple-element.10), calls=%async_computation | async-start | bytes 1310720 | tf_op jit(solution)/shard_map/all_to_all | solution.py:277
  13.4 1.9 %copy-start = (f32[62,96,128]{2,1,0:T(8,128)S(1)}, f32[62,96,128]{2,1,0:T(8,128)}, u32[]{:S(2)}) copy-start(f32[62,96,128]{2,1,0:T(8,128)} %get-tuple-element.11.maps) | copy-start | bytes 9142276
  15.2 1.1 %copy-start.3 = (f32[32,48,96]{2,1,0:T(8,128)S(1)}, f32[32,48,96]{2,1,0:T(8,128)}, u32[]{:S(2)}) copy-start(f32[32,48,96]{2,1,0:T(8,128)} %k_ref.1) | copy-start | bytes 1769476
  32.8 1.2 %copy-start.1 = (f32[30,96,128]{2,1,0:T(8,128)}, f32[30,96,128]{2,1,0:T(8,128)S(1)}, u32[]{:S(2)}) copy-start(f32[30,96,128]{2,1,0:T(8,128)S(1)} %get-tuple-element.14.maps) | copy-start | bytes 4423684
  33.9 7.7 %collective-permute-start = (f32[128,128]{1,0:T(8,128)S(1)}, f32[128,128]{1,0:T(8,128)S(1)}, u32[]{:S(2)}, u32[]{:S(2)}) collective-permute-start(f32[128,128]{1,0:T(8,128)S(1)} %get-tuple-element.13.own_ref), channel_id=1, source_target_pairs={{0,256},{16,272},{32,288},{48,304},{64,320},{80,336},{96,352},{112... | collective-permute-start | bytes 196616 | tf_op jit(solution)/shard_map/ppermute | solution.py:295
  38.6 1.4 %copy-start.2 = (f32[30,96,128]{2,1,0:T(8,128)S(1)}, f32[30,96,128]{2,1,0:T(8,128)}, u32[]{:S(2)}) copy-start(f32[30,96,128]{2,1,0:T(8,128)} %copy-done.1) | copy-start | bytes 4423684

commit v3 on v2

--- a/solution.py
+++ b/solution.py
@@ -36,15 +36,19 @@
 
 
 def compose(later, earlier):
-    lh, ll = split(later)
-    eh, el = extended(earlier)
-    return dot(lh, eh) + (dot(lh, el) + dot(ll, eh))
+    count = later.shape[0]
+    both = dot(
+        jnp.concatenate(split(later), axis=0), jnp.concatenate(extended(earlier), axis=1)
+    )
+    return both[:count, :LANES] + (both[:count, LANES:] + both[count:, :LANES])
 
 
 def carry(rows, following):
-    rh, rl = split(rows)
-    mh, ml = extended(following)
-    return dot_t(rh, mh) + (dot_t(rh, ml) + dot_t(rl, mh))
+    count = rows.shape[0]
+    both = dot_t(
+        jnp.concatenate(split(rows), axis=0), jnp.concatenate(extended(following), axis=0)
+    )
+    return both[:count, :LANES] + (both[:count, LANES:] + both[count:, :LANES])
 
 
 def with_offset(matrix, offset):
@@ -93,11 +97,11 @@
     return jnp.concatenate([top, bottom], axis=0)
 
 
-def summary_kernel(a_hbm, d_hbm, x_hbm, out_ref, maps, a_ref, d_ref, x_ref, sems):
+def summary_kernel(a_hbm, d_hbm, x_hbm, out_ref, a_ref, d_ref, x_ref, maps, sems):
     steps, n = d_ref.shape
     parts = 4
     size = steps // parts
-    copies = [
+    small = [
         pltpu.make_async_copy(d_hbm, d_ref, sems.at[parts]),
         pltpu.make_async_copy(x_hbm, x_ref, sems.at[parts + 1]),
     ]
@@ -105,25 +109,30 @@
     for c in range(parts):
         part = pl.ds(c * size, size)
         blocks.append(pltpu.make_async_copy(a_hbm.at[part], a_ref.at[part], sems.at[c]))
-    for copy in copies[:1] + blocks + copies[1:]:
+    for copy in small[:1] + blocks + small[1:]:
         copy.start()
-    copies[0].wait()
+    small[0].wait()
     offsets = jnp.transpose(d_ref[...])
     for c in range(parts):
         blocks[c].wait()
-        for t in range(c * size, (c + 1) * size):
-            maps[t] = with_offset(a_ref[t], offsets[:, t : t + 1])
-    total = rounds(maps, steps)
-    copies[1].wait()
+        for t in range(c * size, (c + 1) * size, 2):
+            pair = [with_offset(a_ref[k], offsets[:, k : k + 1]) for k in (t, t + 1)]
+            maps[t // 2] = compose(pair[1], pair[0])
+    total = rounds(maps, steps // 2)
+    small[1].wait()
     top, tail = packed(total, x_ref[...])
     for j in range(out_ref.shape[0]):
         out_ref[j, : top.shape[0]] = top
         out_ref[j, top.shape[0] :] = tail
 
 
-def prefix_kernel(k_ref, f_ref, maps, out_ref, rows_ref):
+def prefix_kernel(a_ref, d_ref, k_ref, f_ref, out_ref, maps, rows_ref):
     steps, m, n = k_ref.shape
     feeds = jnp.transpose(f_ref[...])
+    offsets = jnp.transpose(d_ref[...])
+    for t in range(steps):
+        maps[t] = with_offset(a_ref[t], offsets[:, t : t + 1])
+    rounds(maps, steps)
     row, lane = (lax.broadcasted_iota(jnp.int32, (n, LANES), d) for d in (0, 1))
     unit = jnp.where(row == lane, 1.0, 0.0).astype(f32)
 
@@ -151,43 +160,63 @@
         out_ref[at : at + block, LANES:] = low
 
 
-def group_kernel(r_ref, out_ref, maps):
-    count, lines, _ = r_ref.shape
-    n = maps.shape[1]
-    body = lines - 8
-    heads = [
+def heads_of(r_ref, body):
+    count = r_ref.shape[0]
+    return [
         jnp.concatenate([r_ref[j, body + k : body + k + 1] for j in range(count)], axis=0)
         for k in range(3)
     ]
-    offsets = jnp.transpose(heads[0])[:n]
+
+
+def unpack(r_ref, maps):
+    count, lines, _ = r_ref.shape
+    body = lines - 8
+    heads = heads_of(r_ref, body)
+    offsets = jnp.transpose(heads[0])[: maps.shape[1]]
     for j in range(count):
         maps[j] = unpacked(r_ref[j, :body], offsets[:, j : j + 1])
-    out_ref[:n] = rounds(maps, count)
-    for s in range(2):
-        out_ref[n + s * count : n + (s + 1) * count] = heads[1 + s]
-
-
-def inner_kernel(i_ref, maps, out_ref):
+    return heads[1:]
+
+
+def group_kernel(r_ref, out_ref, maps):
+    count, n = r_ref.shape[0], maps.shape[1]
+    starts = unpack(r_ref, maps)
+    total = rounds(maps, count)
+    for j in range(out_ref.shape[0]):
+        out_ref[j, :n] = total
+        for s in range(2):
+            out_ref[j, n + s * count : n + (s + 1) * count] = starts[s]
+
+
+def inner_kernel(i_ref, r_ref, out_ref, maps):
     n = out_ref.shape[0]
     index = i_ref[0]
+    unpack(r_ref, maps)
     row, lane = (lax.broadcasted_iota(jnp.int32, (n, LANES), d) for d in (0, 1))
     held = jnp.where(row == lane, 1.0, 0.0).astype(f32)
-    held = jnp.where((index & 8) != 0, maps[28], held)
-    for bit, first in ((4, 24), (2, 16), (1, 0)):
-        at = first + (index // (2 * bit)) * 2
+    count = r_ref.shape[0]
+    rounds(maps, count)
+    bit = count // 2
+    while bit:
+        at = 2 * count - 2 * (count // bit) + (index // (2 * bit)) * 2
         held = jnp.where((index & bit) != 0, compose(maps[at], held), held)
+        bit //= 2
     out_ref[...] = held
 
 
-def apply_kernel(i_ref, own_ref, other_ref, inner_ref, maps_ref, out_ref):
+def apply_kernel(i_ref, rows_ref, inner_ref, maps_ref, out_ref):
     n = inner_ref.shape[0]
-    second = i_ref[0] >= 16
-    own, other = own_ref[n:], other_ref[n:]
-    halves = jnp.where(second, other, own), jnp.where(second, own, other)
-    start = jnp.concatenate([h[16 * s : 16 * s + 16] for s in (0, 1) for h in halves], axis=0)
+    row = i_ref[0]
+    outer = rows_ref.shape[0]
+    size = (rows_ref.shape[1] - n) // 2
+    start = jnp.concatenate(
+        [rows_ref[k, n + s * size : n + (s + 1) * size] for s in (0, 1) for k in range(outer)],
+        axis=0,
+    )
     lane = lanes_of(start.shape)
     start = jnp.where(lane < n, start, jnp.where(lane == n, 1.0, 0.0))
-    start = jnp.where(second, carry(start, other_ref[:n]), start)
+    for k in range(outer - 1):
+        start = jnp.where(row > k, carry(start, rows_ref[k, :n]), start)
     xh, xl = split(carry(start, inner_ref[...]))
     x = jnp.concatenate(
         [jnp.concatenate([xh, xh], axis=1), jnp.concatenate([xl, jnp.zeros_like(xl)], axis=1)],
@@ -253,57 +282,67 @@
     steps, n, _ = closed_loop.shape
     m = gains.shape[1]
     blocks = lax.axis_size("tm")
-    half = blocks // 2
+    inner, outer = 8, blocks // 8
     shape = jax.ShapeDtypeStruct
     index = lax.axis_index("tm").astype(jnp.int32)
-    inner_index = (index % half).reshape(1)
-    index = index.reshape(1)
+    at_inner, at_outer = (index % inner).reshape(1), (index // inner).reshape(1)
+    near = [[k * inner + j for j in range(inner)] for k in range(outer)]
+    far = [[k * inner + j for k in range(outer)] for j in range(inner)]
     semaphores = pltpu.SemaphoreType.DMA
 
-    payload, maps = call(
+    payload = call(
         summary_kernel,
-        [shape((half, 3 * n // 4 + 8, LANES), f32), shape((2 * steps - 2, n, LANES), f32)],
+        shape((inner, 3 * n // 4 + 8, LANES), f32),
         [HBM] * 3,
         scratch=[
             pltpu.VMEM((steps, n, n), f32),
             pltpu.VMEM((steps, n), f32),
             pltpu.VMEM((2, n), f32),
+            pltpu.VMEM((steps, n, LANES), f32),
             semaphores((6,)),
         ],
         flops=300_000_000,
         limit=60 * 1024 * 1024,
     )(closed_loop, drift_terms, jnp.transpose(initial_states))
-    groups = [[h * half + j for j in range(half)] for h in range(2)]
-    gathered = lax.all_to_all(payload, "tm", 0, 0, tiled=True, axis_index_groups=groups)
+    gathered = lax.all_to_all(payload, "tm", 0, 0, tiled=True, axis_index_groups=near)
 
     rows = (n + m) * steps
     local = call(
         prefix_kernel,
         shape((rows, 2 * LANES), bf16),
-        [VMEM] * 3,
-        scratch=[pltpu.VMEM((rows, LANES), f32)],
+        [VMEM] * 4,
+        scratch=[
+            pltpu.VMEM((2 * steps, n, LANES), f32),
+            pltpu.VMEM((rows, LANES), f32),
+        ],
         flops=500_000_000,
-    )(gains, feedforward, maps)
+    )(closed_loop, drift_terms, gains, feedforward)
     gathered, local = lax.optimization_barrier((gathered, local))
 
-    own, group_maps = call(
+    group = call(
         group_kernel,
-        [shape((n + 2 * half, LANES), f32), shape((2 * half - 2, n, LANES), f32)],
+        shape((outer, n + 2 * inner, LANES), f32),
         [VMEM],
+        scratch=[pltpu.VMEM((2 * inner, n, LANES), f32)],
         flops=150_000_000,
     )(gathered)
-    other = lax.ppermute(own, "tm", [(j, (j + half) % blocks) for j in range(blocks)])
-    inner = call(inner_kernel, shape((n, LANES), f32), [SMEM, VMEM], flops=50_000_000)(
-        inner_index, group_maps
-    )
+    across = lax.all_to_all(group, "tm", 0, 0, tiled=True, axis_index_groups=far)
+    before = call(
+        inner_kernel,
+        shape((n, LANES), f32),
+        [SMEM, VMEM],
+        scratch=[pltpu.VMEM((2 * inner, n, LANES), f32)],
+        flops=150_000_000,
+    )(at_inner, gathered)
+    across, before = lax.optimization_barrier((across, before))
 
     lines = 2 * rows // LANES
     sent = call(
         apply_kernel,
         shape((blocks * lines, LANES), f32),
-        [SMEM] + [VMEM] * 4,
+        [SMEM] + [VMEM] * 3,
         flops=300_000_000,
-    )(index, own, other, inner, local)
+    )(at_outer, across, before, local)
     moved = lax.all_to_all(sent.reshape(blocks, lines, LANES), "tm", 0, 0, tiled=True)
     states, controls = call(
         order_kernel,

time: 82.7 us -> 74.5 us (0.901)
  blocking collectives: 37.8 us -> 33.4 us
  local copies, waits for them, and re-layouts: 5.5 us -> 1.42 us
  Pallas kernels: 13.8 us -> 15.8 us
  starting transfers between devices: 12.8 us -> 11.4 us
    ppermute x1 -> x0, starting transfers between devices: 4.63 us -> none  [body(): lax.ppermute(own, 'tm', [(j, (j + half) % blocks) for j in range(blocks)])]
    all_to_all x1, blocking collectives: 37.8 us -> 33.4 us  [body(): lax.all_to_all(sent.reshape(blocks, lines, LANES), 'tm', 0, 0, tiled=True)]
    unnamed x10 -> x8, local copies, waits for them, and re-layouts: 5.5 us -> 1.42 us
    all_to_all x1 -> x2, starting transfers between devices: 8.14 us -> 11.4 us  [the longest x1 7.12 us: body(): lax.all_to_all(payload, 'tm', 0, 0, tiled=True, axis_index_groups=near)]
    pallas_call x4, Pallas kernels: 10.8 us -> 12.6 us  [the longest x1 5.69 us: body(): call(prefix_kernel, shape((rows, 2 * LANES), bf16), [VMEM] * 4, scratch=[...]
    ppermute x1 -> x0, waiting for transfers between devices: 1.13 us -> none  [body(): lax.ppermute(own, 'tm', [(j, (j + half) % blocks) for j in range(blocks)])]
    all_to_all x1 -> x2, waiting for transfers between devices: 10.7 us -> 11.4 us  [the longest x1 6.14 us: body(): lax.all_to_all(payload, 'tm', 0, 0, tiled=True, axis_index_groups=near)]
  transfers between devices with their start and end apart: 2 -> 2, of which waited for: 2 -> 2; matrix products, arithmetic and copies ran while one was open for 0% -> 0% of each run, Pallas kernels for 6% -> 9%
where the time goes in v3:
time: 74.5 us; the launch traced here: 74.1 us
  blocking collectives  33.4 us (45%)
  Pallas kernels  15.8 us (21%)
  starting transfers between devices  11.4 us (15%)
  waiting for transfers between devices  11.4 us (15%)
  local copies, waits for them, and re-layouts  1.42 us (2%)
    all_to_all x1, blocking collectives, body(): lax.all_to_all(sent.reshape(blocks, lines, LANES), 'tm', 0, 0, tiled=True)  33.4 us
    all_to_all x1, starting transfers between devices, body(): lax.all_to_all(payload, 'tm', 0, 0, tiled=True, axis_index_groups=near)  7.12 us
    all_to_all x1, waiting for transfers between devices, body(): lax.all_to_all(payload, 'tm', 0, 0, tiled=True, axis_index_groups=near)  6.14 us
    pallas_call x1, Pallas kernels, body(): call(prefix_kernel, shape((rows, 2 * LANES), bf16), [VMEM] * 4, scratch=[...  5.69 us
    all_to_all x1, waiting for transfers between devices, body(): lax.all_to_all(group, 'tm', 0, 0, tiled=True, axis_index_groups=far)  5.28 us
    all_to_all x1, starting transfers between devices, body(): lax.all_to_all(group, 'tm', 0, 0, tiled=True, axis_index_groups=far)  4.3 us
    pallas_call x1, Pallas kernels, body(): call(summary_kernel, shape((inner, 3 * n // 4 + 8, LANES), f32), [HBM] *...  4.14 us
    pallas_call x1, Pallas kernels, body(): call(order_kernel, [shape((2 * n, blocks * steps), f32), shape((2 * m, bl...  1.77 us
  transfers between devices with their start and end apart: 2, of which 2 were waited for; matrix products, arithmetic and copies ran while one was open for 0% of the time, Pallas kernels for 9%

profile of v3, /device:TPU:448, one launch (start us, length us, event | category | flops | bytes accessed | tf_op | source)
XLA Modules:
  0.0 74.1 jit_solution(9938019979371460179)
XLA Ops:
  0.6 0.0 copy-start.2
  0.6 0.0 copy-start.3
  0.7 0.0 copy-start.1
  0.7 4.1 %shard_map.68 = f32[8,80,128]{2,1,0:T(8,128)} custom-call(f32[32,96,96]{2,1,0:T(8,128)} %a_ref.1, f32[32,96]{1,0:T(8,128)} %d_ref.1, f32[2,96]{1,0:T(2,128)} %bitcast.7), custom_call_target="tpu_custom_call" | custom-call | flops 300000000 | bytes 4000000 | tf_op jit(solution)/shard_map/pallas_call | solution.py:293
  4.8 7.1 %all-to-all-start = ((f32[8,80,128]{2,1,0:T(8,128)}), f32[8,80,128]{2,1,0:T(8,128)S(1)}, u32[]{:S(2)}, u32[]{:S(2)}) async-start(f32[8,80,128]{2,1,0:T(8,128)} %shard_map.68), calls=%async_computation | async-start | bytes 655360 | tf_op jit(solution)/shard_map/all_to_all | solution.py:307
  11.9 0.0 copy-done.2
  11.9 0.0 copy-done.3
  11.9 0.0 copy-done.1
  12.0 0.0 copy-start
  12.0 1.4 %copy-done = f32[32,96,96]{2,1,0:T(8,128)S(1)} copy-done((f32[32,96,96]{2,1,0:T(8,128)S(1)}, f32[32,96,96]{2,1,0:T(8,128)}, u32[]{:S(2)}) %copy-start) | copy-done | bytes 1179672
  13.4 5.7 %shard_map.69.maps_ref = bf16[4608,256]{1,0:T(8,128)(2,1)S(1)} custom-call(f32[32,96,96]{2,1,0:T(8,128)S(1)} %copy-done, f32[32,96]{1,0:T(8,128)S(1)} %copy-done.2, f32[32,48,96]{2,1,0:T(8,128)S(1)} %copy-done.1, f32[32,48]{1,0:T(8,128)S(1)} %copy-done.3), custom_call_target="tpu_custom_call" | custom-call | flops 500000000 | bytes 4000000 | tf_op jit(solution)/shard_map/pallas_call | solution.py:310
  19.1 6.1 %all-to-all-done.r_ref = f32[8,80,128]{2,1,0:T(8,128)S(1)} async-done(((f32[8,80,128]{2,1,0:T(8,128)}), f32[8,80,128]{2,1,0:T(8,128)S(1)}, u32[]{:S(2)}, u32[]{:S(2)}) %all-to-all-start) | async-done | bytes 327712 | tf_op jit(solution)/shard_map/all_to_all | solution.py:307
  25.2 1.5 %shard_map.70 = f32[4,112,128]{2,1,0:T(8,128)} custom-call(f32[8,80,128]{2,1,0:T(8,128)S(1)} %all-to-all-done.r_ref), custom_call_target="tpu_custom_call" | custom-call | flops 150000000 | bytes 4000000 | tf_op jit(solution)/shard_map/pallas_call | solution.py:322
  26.7 4.3 %all-to-all-start.1 = ((f32[4,112,128]{2,1,0:T(8,128)}), f32[4,112,128]{2,1,0:T(8,128)S(1)}, u32[]{:S(2)}, u32[]{:S(2)}) async-start(f32[4,112,128]{2,1,0:T(8,128)} %shard_map.70), calls=%async_computation.1 | async-start | bytes 458752 | tf_op jit(solution)/shard_map/all_to_all | solution.py:329
  31.0 1.2 %shard_map.71.inner_ref = f32[96,128]{1,0:T(8,128)S(1)} custom-call(s32[1]{0:T(128)} %bitcast.2.i_ref, f32[8,80,128]{2,1,0:T(8,128)S(1)} %all-to-all-done.r_ref), custom_call_target="tpu_custom_call" | custom-call | flops 150000000 | bytes 4000000 | tf_op jit(solution)/shard_map/pallas_call | solution.py:330
  32.3 5.3 %all-to-all-done.1.rows_ref = f32[4,112,128]{2,1,0:T(8,128)S(1)} async-done(((f32[4,112,128]{2,1,0:T(8,128)}), f32[4,112,128]{2,1,0:T(8,128)S(1)}, u32[]{:S(2)}, u32[]{:S(2)}) %all-to-all-start.1) | async-done | bytes 229408 | tf_op jit(solution)/shard_map/all_to_all | solution.py:329
  37.5 1.4 %shard_map.72 = f32[2304,128]{1,0:T(8,128)S(1)} custom-call(s32[1]{0:T(128)} %bitcast.i_ref, f32[4,112,128]{2,1,0:T(8,128)S(1)} %all-to-all-done.1.rows_ref, f32[96,128]{1,0:T(8,128)S(1)} %shard_map.71.inner_ref, bf16[4608,256]{1,0:T(8,128)(2,1)S(1)} %shard_map.69.maps_ref), custom_call_target="tpu_custom_call" | custom-call | flops 300000000 | bytes 4000000 | tf_op jit(solution)/shard_map/pallas_call | solution.py:340
  39.0 33.4 %all_to_all.15.r_ref = f32[32,72,128]{2,1,0:T(8,128)S(1)} all-to-all(f32[32,72,128]{2,1,0:T(8,128)S(1)} %bitcast.6), channel_id=1, replica_groups=mesh['tm'=32,'scen'=16] {'tm'}, dimensions={0} | all-to-all | bytes 2359296 | tf_op jit(solution)/shard_map/all_to_all | solution.py:346
  72.4 1.8 %shard_map.73 = (f32[192,1024]{1,0:T(8,128)}, f32[96,1024]{1,0:T(8,128)}) custom-call(f32[32,72,128]{2,1,0:T(8,128)S(1)} %all_to_all.15.r_ref), custom_call_target="tpu_custom_call" | custom-call | flops 1000000 | bytes 4000000 | tf_op jit(solution)/shard_map/pallas_call | solution.py:347
Async XLA Ops:
  0.6 11.3 %copy-start.2 = (f32[32,96]{1,0:T(8,128)S(1)}, f32[32,96]{1,0:T(8,128)}, u32[]{:S(2)}) copy-start(f32[32,96]{1,0:T(8,128)} %d_ref.1) | copy-start | bytes 36868
  0.6 11.3 %copy-start.3 = (f32[32,48]{1,0:T(8,128)S(1)}, f32[32,48]{1,0:T(8,128)}, u32[]{:S(2)}) copy-start(f32[32,48]{1,0:T(8,128)} %f_ref.1) | copy-start | bytes 18436
  0.7 11.3 %copy-start.1 = (f32[32,48,96]{2,1,0:T(8,128)S(1)}, f32[32,48,96]{2,1,0:T(8,128)}, u32[]{:S(2)}) copy-start(f32[32,48,96]{2,1,0:T(8,128)} %k_ref.1) | copy-start | bytes 1769476
  4.8 20.4 %all-to-all-start = ((f32[8,80,128]{2,1,0:T(8,128)}), f32[8,80,128]{2,1,0:T(8,128)S(1)}, u32[]{:S(2)}, u32[]{:S(2)}) async-start(f32[8,80,128]{2,1,0:T(8,128)} %shard_map.68), calls=%async_computation | async-start | bytes 655360 | tf_op jit(solution)/shard_map/all_to_all | solution.py:307
  12.0 1.4 %copy-start = (f32[32,96,96]{2,1,0:T(8,128)S(1)}, f32[32,96,96]{2,1,0:T(8,128)}, u32[]{:S(2)}) copy-start(f32[32,96,96]{2,1,0:T(8,128)} %a_ref.1) | copy-start | bytes 3538948
  26.7 10.8 %all-to-all-start.1 = ((f32[4,112,128]{2,1,0:T(8,128)}), f32[4,112,128]{2,1,0:T(8,128)S(1)}, u32[]{:S(2)}, u32[]{:S(2)}) async-start(f32[4,112,128]{2,1,0:T(8,128)} %shard_map.70), calls=%async_computation.1 | async-start | bytes 458752 | tf_op jit(solution)/shard_map/all_to_all | solution.py:329

commit v4 on v3

--- a/solution.py
+++ b/solution.py
@@ -23,22 +23,22 @@
     return lax.dot_general(a, b, (((1,), (1,)), ((), ())), preferred_element_type=f32)
 
 
-def extended(x):
+def extended(x, lane_of=0):
     n = x.shape[0]
     high, low = split(x)
     shape = (LANES - n, LANES)
     row, lane = (lax.broadcasted_iota(jnp.int32, shape, d) for d in (0, 1))
-    one = jnp.where((row == 0) & (lane >= n), 1.0, 0.0).astype(bf16)
+    one = jnp.where((row == lane_of) & (lane >= n), 1.0, 0.0).astype(bf16)
     return (
         jnp.concatenate([high, one], axis=0),
         jnp.concatenate([low, jnp.zeros(shape, bf16)], axis=0),
     )
 
 
-def compose(later, earlier):
+def compose(later, earlier, lane_of=0):
     count = later.shape[0]
     both = dot(
-        jnp.concatenate(split(later), axis=0), jnp.concatenate(extended(earlier), axis=1)
+        jnp.concatenate(split(later), axis=0), jnp.concatenate(extended(earlier, lane_of), axis=1)
     )
     return both[:count, :LANES] + (both[:count, LANES:] + both[count:, :LANES])
 
@@ -51,18 +51,28 @@
     return both[:count, :LANES] + (both[:count, LANES:] + both[count:, :LANES])
 
 
-def with_offset(matrix, offset):
-    wide = jnp.broadcast_to(offset, (matrix.shape[0], LANES - matrix.shape[1]))
-    return jnp.concatenate([matrix, wide], axis=1)
-
-
-def rounds(maps, count, at=0):
+def columns(rows, n):
+    count, width = rows.shape
+    if width < n:
+        rows = jnp.pad(rows, ((0, 0), (0, n - width)))
+    turned = jnp.transpose(rows)
+    if count < LANES - n:
+        turned = jnp.pad(turned, ((0, 0), (0, LANES - n - count)))
+    return turned
+
+
+def with_offsets(matrix, offsets):
+    return jnp.concatenate([matrix, offsets[: matrix.shape[0]]], axis=1)
+
+
+def rounds(maps, count, size=1):
+    at = 0
     while count > 2:
         end = at + count
         for k in range(count // 2):
-            maps[end + k] = compose(maps[at + 2 * k + 1], maps[at + 2 * k])
-        at, count = end, count // 2
-    return compose(maps[at + 1], maps[at])
+            maps[end + k] = compose(maps[at + 2 * k + 1], maps[at + 2 * k], (2 * k + 1) * size)
+        at, count, size = end, count // 2, 2 * size
+    return compose(maps[at + 1], maps[at], size)
 
 
 def lanes_of(shape):
@@ -87,7 +97,6 @@
     body = lines.shape[0]
     spare = body // 3
     n = body + spare
-    offset = jnp.broadcast_to(offset, (n, LANES))
     lane = lanes_of((spare, LANES))
     bottom = offset[body:]
     for c in range(3):
@@ -99,7 +108,7 @@
 
 def summary_kernel(a_hbm, d_hbm, x_hbm, out_ref, a_ref, d_ref, x_ref, maps, sems):
     steps, n = d_ref.shape
-    parts = 4
+    parts = 2
     size = steps // parts
     small = [
         pltpu.make_async_copy(d_hbm, d_ref, sems.at[parts]),
@@ -112,13 +121,13 @@
     for copy in small[:1] + blocks + small[1:]:
         copy.start()
     small[0].wait()
-    offsets = jnp.transpose(d_ref[...])
+    offsets = columns(d_ref[...], n)
     for c in range(parts):
         blocks[c].wait()
         for t in range(c * size, (c + 1) * size, 2):
-            pair = [with_offset(a_ref[k], offsets[:, k : k + 1]) for k in (t, t + 1)]
-            maps[t // 2] = compose(pair[1], pair[0])
-    total = rounds(maps, steps // 2)
+            pair = [with_offsets(a_ref[k], offsets) for k in (t, t + 1)]
+            maps[t // 2] = compose(pair[1], pair[0], t + 1)
+    total = rounds(maps, steps // 2, 2)
     small[1].wait()
     top, tail = packed(total, x_ref[...])
     for j in range(out_ref.shape[0]):
@@ -128,10 +137,10 @@
 
 def prefix_kernel(a_ref, d_ref, k_ref, f_ref, out_ref, maps, rows_ref):
     steps, m, n = k_ref.shape
-    feeds = jnp.transpose(f_ref[...])
-    offsets = jnp.transpose(d_ref[...])
+    feeds = columns(f_ref[...], n)
+    offsets = columns(d_ref[...], n)
     for t in range(steps):
-        maps[t] = with_offset(a_ref[t], offsets[:, t : t + 1])
+        maps[t] = with_offsets(a_ref[t], offsets)
     rounds(maps, steps)
     row, lane = (lax.broadcasted_iota(jnp.int32, (n, LANES), d) for d in (0, 1))
     unit = jnp.where(row == lane, 1.0, 0.0).astype(f32)
@@ -149,10 +158,10 @@
         at = 2 * steps - 2 * (steps // size)
         put(size, maps[at])
         for t in range(2 * size, steps, 2 * size):
-            put(t + size, compose(maps[at + t // size], get(t)))
+            put(t + size, compose(maps[at + t // size], get(t), t))
     for t in range(steps):
-        gain = with_offset(-k_ref[t], feeds[:, t : t + 1])
-        rows_ref[pl.ds(n * steps + t, m, stride=steps)] = compose(gain, get(t))
+        gain = with_offsets(-k_ref[t], feeds)
+        rows_ref[pl.ds(n * steps + t, m, stride=steps)] = compose(gain, get(t), t)
     block = 512
     for at in range(0, (n + m) * steps, block):
         high, low = split(rows_ref[at : at + block])
@@ -170,11 +179,12 @@
 
 def unpack(r_ref, maps):
     count, lines, _ = r_ref.shape
+    n = maps.shape[1]
     body = lines - 8
     heads = heads_of(r_ref, body)
-    offsets = jnp.transpose(heads[0])[: maps.shape[1]]
+    offsets = with_offsets(jnp.zeros((n, n), f32), columns(heads[0][:, :n], n))
     for j in range(count):
-        maps[j] = unpacked(r_ref[j, :body], offsets[:, j : j + 1])
+        maps[j] = unpacked(r_ref[j, :body], offsets)
     return heads[1:]
 
 
@@ -198,8 +208,9 @@
     rounds(maps, count)
     bit = count // 2
     while bit:
-        at = 2 * count - 2 * (count // bit) + (index // (2 * bit)) * 2
-        held = jnp.where((index & bit) != 0, compose(maps[at], held), held)
+        pair = index // (2 * bit)
+        at = 2 * count - 2 * (count // bit) + pair * 2
+        held = jnp.where((index & bit) != 0, compose(maps[at], held, pair * 2 * bit), held)
         bit //= 2
     out_ref[...] = held
 
@@ -215,9 +226,10 @@
     )
     lane = lanes_of(start.shape)
     start = jnp.where(lane < n, start, jnp.where(lane == n, 1.0, 0.0))
-    for k in range(outer - 1):
-        start = jnp.where(row > k, carry(start, rows_ref[k, :n]), start)
-    xh, xl = split(carry(start, inner_ref[...]))
+    first = jnp.where(row > 1, compose(rows_ref[1, :n], rows_ref[0, :n]), rows_ref[0, :n])
+    second = jnp.where(row > 2, compose(inner_ref[...], rows_ref[2, :n]), inner_ref[...])
+    start = jnp.where(row > 0, carry(start, first), start)
+    xh, xl = split(carry(start, second))
     x = jnp.concatenate(
         [jnp.concatenate([xh, xh], axis=1), jnp.concatenate([xl, jnp.zeros_like(xl)], axis=1)],
         axis=0,

time: 74.5 us -> 73.8 us (level)
  Pallas kernels: 15.8 us -> 14.9 us
where the time goes in v4:
time: 73.8 us; the launch traced here: 73.4 us
  blocking collectives  33.4 us (45%)
  Pallas kernels  14.9 us (20%)
  waiting for transfers between devices  11.6 us (16%)
  starting transfers between devices  11.4 us (15%)
  local copies, waits for them, and re-layouts  1.42 us (2%)
    all_to_all x1, blocking collectives, body(): lax.all_to_all(sent.reshape(blocks, lines, LANES), 'tm', 0, 0, tiled=True)  33.4 us
    all_to_all x1, starting transfers between devices, body(): lax.all_to_all(payload, 'tm', 0, 0, tiled=True, axis_index_groups=near)  7.1 us
    all_to_all x1, waiting for transfers between devices, body(): lax.all_to_all(payload, 'tm', 0, 0, tiled=True, axis_index_groups=near)  6.25 us
    pallas_call x1, Pallas kernels, body(): call(prefix_kernel, shape((rows, 2 * LANES), bf16), [VMEM] * 4, scratch=[...  5.59 us
    all_to_all x1, waiting for transfers between devices, body(): lax.all_to_all(group, 'tm', 0, 0, tiled=True, axis_index_groups=far)  5.4 us
    all_to_all x1, starting transfers between devices, body(): lax.all_to_all(group, 'tm', 0, 0, tiled=True, axis_index_groups=far)  4.3 us
    pallas_call x1, Pallas kernels, body(): call(summary_kernel, shape((inner, 3 * n // 4 + 8, LANES), f32), [HBM] *...  3.63 us
    pallas_call x1, Pallas kernels, body(): call(order_kernel, [shape((2 * n, blocks * steps), f32), shape((2 * m, bl...  1.77 us
  transfers between devices with their start and end apart: 2, of which 2 were waited for; matrix products, arithmetic and copies ran while one was open for 0% of the time, Pallas kernels for 9%

profile of v4, /device:TPU:448, one launch (start us, length us, event | category | flops | bytes accessed | tf_op | source)
XLA Modules:
  0.0 73.4 jit_solution(6577598277489948786)
XLA Ops:
  0.6 0.0 copy-start.2
  0.6 0.0 copy-start.3
  0.7 0.0 copy-start.1
  0.7 3.6 %shard_map.68 = f32[8,80,128]{2,1,0:T(8,128)} custom-call(f32[32,96,96]{2,1,0:T(8,128)} %a_ref.1, f32[32,96]{1,0:T(8,128)} %d_ref.1, f32[2,96]{1,0:T(2,128)} %bitcast.7), custom_call_target="tpu_custom_call" | custom-call | flops 300000000 | bytes 4000000 | tf_op jit(solution)/shard_map/pallas_call | solution.py:305
  4.3 7.1 %all-to-all-start = ((f32[8,80,128]{2,1,0:T(8,128)}), f32[8,80,128]{2,1,0:T(8,128)S(1)}, u32[]{:S(2)}, u32[]{:S(2)}) async-start(f32[8,80,128]{2,1,0:T(8,128)} %shard_map.68), calls=%async_computation | async-start | bytes 655360 | tf_op jit(solution)/shard_map/all_to_all | solution.py:319
  11.4 0.0 copy-done.2
  11.4 0.0 copy-done.3
  11.4 0.0 copy-done.1
  11.4 0.0 copy-start
  11.4 1.4 %copy-done = f32[32,96,96]{2,1,0:T(8,128)S(1)} copy-done((f32[32,96,96]{2,1,0:T(8,128)S(1)}, f32[32,96,96]{2,1,0:T(8,128)}, u32[]{:S(2)}) %copy-start) | copy-done | bytes 1179672
  12.8 5.6 %shard_map.69.maps_ref = bf16[4608,256]{1,0:T(8,128)(2,1)S(1)} custom-call(f32[32,96,96]{2,1,0:T(8,128)S(1)} %copy-done, f32[32,96]{1,0:T(8,128)S(1)} %copy-done.2, f32[32,48,96]{2,1,0:T(8,128)S(1)} %copy-done.1, f32[32,48]{1,0:T(8,128)S(1)} %copy-done.3), custom_call_target="tpu_custom_call" | custom-call | flops 500000000 | bytes 4000000 | tf_op jit(solution)/shard_map/pallas_call | solution.py:322
  18.4 6.3 %all-to-all-done.r_ref = f32[8,80,128]{2,1,0:T(8,128)S(1)} async-done(((f32[8,80,128]{2,1,0:T(8,128)}), f32[8,80,128]{2,1,0:T(8,128)S(1)}, u32[]{:S(2)}, u32[]{:S(2)}) %all-to-all-start) | async-done | bytes 327712 | tf_op jit(solution)/shard_map/all_to_all | solution.py:319
  24.7 1.4 %shard_map.70 = f32[4,112,128]{2,1,0:T(8,128)} custom-call(f32[8,80,128]{2,1,0:T(8,128)S(1)} %all-to-all-done.r_ref), custom_call_target="tpu_custom_call" | custom-call | flops 150000000 | bytes 4000000 | tf_op jit(solution)/shard_map/pallas_call | solution.py:334
  26.1 4.3 %all-to-all-start.1 = ((f32[4,112,128]{2,1,0:T(8,128)}), f32[4,112,128]{2,1,0:T(8,128)S(1)}, u32[]{:S(2)}, u32[]{:S(2)}) async-start(f32[4,112,128]{2,1,0:T(8,128)} %shard_map.70), calls=%async_computation.1 | async-start | bytes 458752 | tf_op jit(solution)/shard_map/all_to_all | solution.py:341
  30.4 1.1 %shard_map.71.inner_ref = f32[96,128]{1,0:T(8,128)S(1)} custom-call(s32[1]{0:T(128)} %bitcast.2.i_ref, f32[8,80,128]{2,1,0:T(8,128)S(1)} %all-to-all-done.r_ref), custom_call_target="tpu_custom_call" | custom-call | flops 150000000 | bytes 4000000 | tf_op jit(solution)/shard_map/pallas_call | solution.py:342
  31.5 5.4 %all-to-all-done.1.rows_ref = f32[4,112,128]{2,1,0:T(8,128)S(1)} async-done(((f32[4,112,128]{2,1,0:T(8,128)}), f32[4,112,128]{2,1,0:T(8,128)S(1)}, u32[]{:S(2)}, u32[]{:S(2)}) %all-to-all-start.1) | async-done | bytes 229408 | tf_op jit(solution)/shard_map/all_to_all | solution.py:341
  36.9 1.4 %shard_map.72 = f32[2304,128]{1,0:T(8,128)S(1)} custom-call(s32[1]{0:T(128)} %bitcast.i_ref, f32[4,112,128]{2,1,0:T(8,128)S(1)} %all-to-all-done.1.rows_ref, f32[96,128]{1,0:T(8,128)S(1)} %shard_map.71.inner_ref, bf16[4608,256]{1,0:T(8,128)(2,1)S(1)} %shard_map.69.maps_ref), custom_call_target="tpu_custom_call" | custom-call | flops 300000000 | bytes 4000000 | tf_op jit(solution)/shard_map/pallas_call | solution.py:352
  38.3 33.4 %all_to_all.15.r_ref = f32[32,72,128]{2,1,0:T(8,128)S(1)} all-to-all(f32[32,72,128]{2,1,0:T(8,128)S(1)} %bitcast.6), channel_id=1, replica_groups=mesh['tm'=32,'scen'=16] {'tm'}, dimensions={0} | all-to-all | bytes 2359296 | tf_op jit(solution)/shard_map/all_to_all | solution.py:358
  71.6 1.8 %shard_map.73 = (f32[192,1024]{1,0:T(8,128)}, f32[96,1024]{1,0:T(8,128)}) custom-call(f32[32,72,128]{2,1,0:T(8,128)S(1)} %all_to_all.15.r_ref), custom_call_target="tpu_custom_call" | custom-call | flops 1000000 | bytes 4000000 | tf_op jit(solution)/shard_map/pallas_call | solution.py:359
Async XLA Ops:
  0.6 10.8 %copy-start.2 = (f32[32,96]{1,0:T(8,128)S(1)}, f32[32,96]{1,0:T(8,128)}, u32[]{:S(2)}) copy-start(f32[32,96]{1,0:T(8,128)} %d_ref.1) | copy-start | bytes 36868
  0.6 10.8 %copy-start.3 = (f32[32,48]{1,0:T(8,128)S(1)}, f32[32,48]{1,0:T(8,128)}, u32[]{:S(2)}) copy-start(f32[32,48]{1,0:T(8,128)} %f_ref.1) | copy-start | bytes 18436
  0.7 10.8 %copy-start.1 = (f32[32,48,96]{2,1,0:T(8,128)S(1)}, f32[32,48,96]{2,1,0:T(8,128)}, u32[]{:S(2)}) copy-start(f32[32,48,96]{2,1,0:T(8,128)} %k_ref.1) | copy-start | bytes 1769476
  4.3 20.4 %all-to-all-start = ((f32[8,80,128]{2,1,0:T(8,128)}), f32[8,80,128]{2,1,0:T(8,128)S(1)}, u32[]{:S(2)}, u32[]{:S(2)}) async-start(f32[8,80,128]{2,1,0:T(8,128)} %shard_map.68), calls=%async_computation | async-start | bytes 655360 | tf_op jit(solution)/shard_map/all_to_all | solution.py:319
  11.4 1.4 %copy-start = (f32[32,96,96]{2,1,0:T(8,128)S(1)}, f32[32,96,96]{2,1,0:T(8,128)}, u32[]{:S(2)}) copy-start(f32[32,96,96]{2,1,0:T(8,128)} %a_ref.1) | copy-start | bytes 3538948
  26.1 10.8 %all-to-all-start.1 = ((f32[4,112,128]{2,1,0:T(8,128)}), f32[4,112,128]{2,1,0:T(8,128)S(1)}, u32[]{:S(2)}, u32[]{:S(2)}) async-start(f32[4,112,128]{2,1,0:T(8,128)} %shard_map.70), calls=%async_computation.1 | async-start | bytes 458752 | tf_op jit(solution)/shard_map/all_to_all | solution.py:341

commit v5 on v4

--- a/solution.py
+++ b/solution.py
@@ -135,7 +135,7 @@
         out_ref[j, top.shape[0] :] = tail
 
 
-def prefix_kernel(a_ref, d_ref, k_ref, f_ref, out_ref, maps, rows_ref):
+def prefix_kernel(i_ref, a_ref, d_ref, k_ref, f_ref, out_ref, maps, rows_ref):
     steps, m, n = k_ref.shape
     feeds = columns(f_ref[...], n)
     offsets = columns(d_ref[...], n)
@@ -162,11 +162,13 @@
     for t in range(steps):
         gain = with_offsets(-k_ref[t], feeds)
         rows_ref[pl.ds(n * steps + t, m, stride=steps)] = compose(gain, get(t), t)
-    block = 512
-    for at in range(0, (n + m) * steps, block):
-        high, low = split(rows_ref[at : at + block])
-        out_ref[at : at + block, :LANES] = high
-        out_ref[at : at + block, LANES:] = low
+    turned = [pl.multiple_of((i_ref[0] + k) % 4 * steps, steps) for k in range(4)]
+    for at in range(0, (n + m) * steps, LANES):
+        high, low = split(rows_ref[at : at + LANES])
+        for k in range(4):
+            part = slice(k * steps, (k + 1) * steps)
+            out_ref[pl.ds(at + turned[k], steps), :LANES] = high[part]
+            out_ref[pl.ds(at + turned[k], steps), LANES:] = low[part]
 
 
 def heads_of(r_ref, body):
@@ -188,31 +190,24 @@
     return heads[1:]
 
 
-def group_kernel(r_ref, out_ref, maps):
+def group_kernel(i_ref, r_ref, out_ref, inner_ref, maps):
     count, n = r_ref.shape[0], maps.shape[1]
+    index = i_ref[0]
     starts = unpack(r_ref, maps)
     total = rounds(maps, count)
-    for j in range(out_ref.shape[0]):
-        out_ref[j, :n] = total
-        for s in range(2):
-            out_ref[j, n + s * count : n + (s + 1) * count] = starts[s]
-
-
-def inner_kernel(i_ref, r_ref, out_ref, maps):
-    n = out_ref.shape[0]
-    index = i_ref[0]
-    unpack(r_ref, maps)
     row, lane = (lax.broadcasted_iota(jnp.int32, (n, LANES), d) for d in (0, 1))
     held = jnp.where(row == lane, 1.0, 0.0).astype(f32)
-    count = r_ref.shape[0]
-    rounds(maps, count)
     bit = count // 2
     while bit:
         pair = index // (2 * bit)
         at = 2 * count - 2 * (count // bit) + pair * 2
         held = jnp.where((index & bit) != 0, compose(maps[at], held, pair * 2 * bit), held)
         bit //= 2
-    out_ref[...] = held
+    inner_ref[...] = held
+    for j in range(out_ref.shape[0]):
+        out_ref[j, :n] = total
+        for s in range(2):
+            out_ref[j, n + s * count : n + (s + 1) * count] = starts[s]
 
 
 def apply_kernel(i_ref, rows_ref, inner_ref, maps_ref, out_ref):
@@ -255,10 +250,11 @@
     for g in range(8):
         parts = [r_ref[4 * g + b] for b in range(4)]
         for a in range(4):
-            value = None
-            for b in range(4):
-                moved = parts[b] if a == b else pltpu.roll(parts[b], 32 * ((b - a) % 4), 1)
-                value = moved if value is None else jnp.where(lane == b, moved, value)
+            value = parts[0]
+            for b in range(1, 4):
+                value = jnp.where(lane == (a + b) % 4, parts[b], value)
+            if a:
+                value = pltpu.roll(value, LANES - 32 * a, 1)
             tile_ref[g, pl.ds(a, lines, stride=4)] = value
         across = pl.ds(g * LANES, LANES)
         for k, (rows, to) in enumerate(
@@ -296,8 +292,8 @@
     blocks = lax.axis_size("tm")
     inner, outer = 8, blocks // 8
     shape = jax.ShapeDtypeStruct
-    index = lax.axis_index("tm").astype(jnp.int32)
-    at_inner, at_outer = (index % inner).reshape(1), (index // inner).reshape(1)
+    index = lax.axis_index("tm").astype(jnp.int32).reshape(1)
+    at_inner, at_outer = index % inner, index // inner
     near = [[k * inner + j for j in range(inner)] for k in range(outer)]
     far = [[k * inner + j for k in range(outer)] for j in range(inner)]
     semaphores = pltpu.SemaphoreType.DMA
@@ -322,31 +318,25 @@
     local = call(
         prefix_kernel,
         shape((rows, 2 * LANES), bf16),
-        [VMEM] * 4,
+        [SMEM] + [VMEM] * 4,
         scratch=[
             pltpu.VMEM((2 * steps, n, LANES), f32),
             pltpu.VMEM((rows, LANES), f32),
         ],
         flops=500_000_000,
-    )(closed_loop, drift_terms, gains, feedforward)
-    gathered, local = lax.optimization_barrier((gathered, local))
-
-    group = call(
+    )(index, closed_loop, drift_terms, gains, feedforward)
+    gathered, local, at_inner, at_outer = lax.optimization_barrier(
+        (gathered, local, at_inner, at_outer)
+    )
+
+    group, before = call(
         group_kernel,
-        shape((outer, n + 2 * inner, LANES), f32),
-        [VMEM],
-        scratch=[pltpu.VMEM((2 * inner, n, LANES), f32)],
-        flops=150_000_000,
-    )(gathered)
-    across = lax.all_to_all(group, "tm", 0, 0, tiled=True, axis_index_groups=far)
-    before = call(
-        inner_kernel,
-        shape((n, LANES), f32),
+        [shape((outer, n + 2 * inner, LANES), f32), shape((n, LANES), f32)],
         [SMEM, VMEM],
         scratch=[pltpu.VMEM((2 * inner, n, LANES), f32)],
         flops=150_000_000,
     )(at_inner, gathered)
-    across, before = lax.optimization_barrier((across, before))
+    across = lax.all_to_all(group, "tm", 0, 0, tiled=True, axis_index_groups=far)
 
     lines = 2 * rows // LANES
     sent = call(

time: 73.8 us -> 72.6 us (0.984)
  blocking collectives: 33.4 us -> 43.9 us
  waiting for transfers between devices: 11.6 us -> 6.19 us
  starting transfers between devices: 11.4 us -> 7.1 us
  Pallas kernels: 14.9 us -> 13 us
    all_to_all x0 -> x1, blocking collectives: none -> 10.6 us  [body(): lax.all_to_all(group, 'tm', 0, 0, tiled=True, axis_index_groups=far)]
    all_to_all x1 -> x0, waiting for transfers between devices: 5.4 us -> none  [body(): lax.all_to_all(group, 'tm', 0, 0, tiled=True, axis_index_groups=far)]
    all_to_all x1 -> x0, starting transfers between devices: 4.3 us -> none  [body(): lax.all_to_all(group, 'tm', 0, 0, tiled=True, axis_index_groups=far)]
    pallas_call x3 -> x2, Pallas kernels: 8.1 us -> 6.76 us  [the longest x1 5.65 us: body(): call(prefix_kernel, shape((rows, 2 * LANES), bf16), [SMEM] + [VMEM] * 4,...]
  transfers between devices with their start and end apart: 2 -> 1, of which waited for: 2 -> 1; matrix products, arithmetic and copies ran while one was open for 0% -> 0% of each run, Pallas kernels for 9% -> 8%
where the time goes in v5:
time: 72.6 us; the launch traced here: 72.3 us
  blocking collectives  43.9 us (60%)
  Pallas kernels  13 us (18%)
  starting transfers between devices  7.1 us (10%)
  waiting for transfers between devices  6.19 us (9%)
  local copies, waits for them, and re-layouts  1.42 us (2%)
    all_to_all x1, blocking collectives, body(): lax.all_to_all(sent.reshape(blocks, lines, LANES), 'tm', 0, 0, tiled=True)  33.3 us
    all_to_all x1, blocking collectives, body(): lax.all_to_all(group, 'tm', 0, 0, tiled=True, axis_index_groups=far)  10.6 us
    all_to_all x1, starting transfers between devices, body(): lax.all_to_all(payload, 'tm', 0, 0, tiled=True, axis_index_groups=near)  7.1 us
    all_to_all x1, waiting for transfers between devices, body(): lax.all_to_all(payload, 'tm', 0, 0, tiled=True, axis_index_groups=near)  6.19 us
    pallas_call x1, Pallas kernels, body(): call(prefix_kernel, shape((rows, 2 * LANES), bf16), [SMEM] + [VMEM] * 4,...  5.65 us
    pallas_call x1, Pallas kernels, body(): call(summary_kernel, shape((inner, 3 * n // 4 + 8, LANES), f32), [HBM] *...  3.63 us
  transfers between devices with their start and end apart: 1, of which 1 were waited for; matrix products, arithmetic and copies ran while one was open for 0% of the time, Pallas kernels for 8%

profile of v5, /device:TPU:448, one launch (start us, length us, event | category | flops | bytes accessed | tf_op | source)
XLA Modules:
  0.0 72.3 jit_solution(10578950113623836522)
XLA Ops:
  0.6 0.0 copy-start.2
  0.6 0.0 copy-start.3
  0.7 0.0 copy-start.1
  0.7 3.6 %shard_map.68 = f32[8,80,128]{2,1,0:T(8,128)} custom-call(f32[32,96,96]{2,1,0:T(8,128)} %a_ref.1, f32[32,96]{1,0:T(8,128)} %d_ref.1, f32[2,96]{1,0:T(2,128)} %bitcast.6), custom_call_target="tpu_custom_call" | custom-call | flops 300000000 | bytes 4000000 | tf_op jit(solution)/shard_map/pallas_call | solution.py:301
  4.3 7.1 %all-to-all-start = ((f32[8,80,128]{2,1,0:T(8,128)}), f32[8,80,128]{2,1,0:T(8,128)S(1)}, u32[]{:S(2)}, u32[]{:S(2)}) async-start(f32[8,80,128]{2,1,0:T(8,128)} %shard_map.68), calls=%async_computation | async-start | bytes 655360 | tf_op jit(solution)/shard_map/all_to_all | solution.py:315
  11.4 0.0 copy-done.2
  11.4 0.0 copy-done.3
  11.4 0.0 copy-done.1
  11.4 0.0 copy-start
  11.4 1.4 %copy-done = f32[32,96,96]{2,1,0:T(8,128)S(1)} copy-done((f32[32,96,96]{2,1,0:T(8,128)S(1)}, f32[32,96,96]{2,1,0:T(8,128)}, u32[]{:S(2)}) %copy-start) | copy-done | bytes 1179672
  12.8 5.6 %shard_map.69.maps_ref = bf16[4608,256]{1,0:T(8,128)(2,1)S(1)} custom-call(s32[1]{0:T(128)} %bitcast.1.i_ref, f32[32,96,96]{2,1,0:T(8,128)S(1)} %copy-done, f32[32,96]{1,0:T(8,128)S(1)} %copy-done.2, f32[32,48,96]{2,1,0:T(8,128)S(1)} %copy-done.1, f32[32,48]{1,0:T(8,128)S(1)} %copy-done.3), custom_call_target="tpu_custom_call" | custom-call | flops 500000000 | bytes 4000000 | tf_op jit(solution)/shard_map/pallas_call | solution.py:318
  18.5 6.2 %all-to-all-done.r_ref = f32[8,80,128]{2,1,0:T(8,128)S(1)} async-done(((f32[8,80,128]{2,1,0:T(8,128)}), f32[8,80,128]{2,1,0:T(8,128)S(1)}, u32[]{:S(2)}, u32[]{:S(2)}) %all-to-all-start) | async-done | bytes 327712 | tf_op jit(solution)/shard_map/all_to_all | solution.py:315
  24.7 1.1 %shard_map.70 = (f32[4,112,128]{2,1,0:T(8,128)S(1)}, f32[96,128]{1,0:T(8,128)S(1)}) custom-call(s32[1]{0:T(128)S(6)} %select_n.12.i_ref, f32[8,80,128]{2,1,0:T(8,128)S(1)} %all-to-all-done.r_ref), custom_call_target="tpu_custom_call" | custom-call | flops 150000000 | bytes 4000000 | tf_op jit(solution)/shard_map/pallas_call | solution.py:332
  25.8 10.6 %all_to_all.15.rows_ref = f32[4,112,128]{2,1,0:T(8,128)S(1)} all-to-all(f32[4,112,128]{2,1,0:T(8,128)S(1)} %get-tuple-element.13), channel_id=1, replica_groups={{0,128,256,384},{16,144,272,400},{32,160,288,416},{48,176,304,432},{64,..., dimensions={0} | all-to-all | bytes 458752 | tf_op jit(solution)/shard_map/all_to_all | solution.py:339
  36.4 1.4 %shard_map.71 = f32[2304,128]{1,0:T(8,128)S(1)} custom-call(s32[1]{0:T(128)S(6)} %select_n.13.i_ref, f32[4,112,128]{2,1,0:T(8,128)S(1)} %all_to_all.15.rows_ref, f32[96,128]{1,0:T(8,128)S(1)} %get-tuple-element.14.inner_ref, bf16[4608,256]{1,0:T(8,128)(2,1)S(1)} %shard_map.69.maps_ref), custom_call_target="tpu_custom_call" | custom-call | flops 300000000 | bytes 4000000 | tf_op jit(solution)/shard_map/pallas_call | solution.py:342
  37.8 33.3 %all_to_all.16.r_ref = f32[32,72,128]{2,1,0:T(8,128)S(1)} all-to-all(f32[32,72,128]{2,1,0:T(8,128)S(1)} %bitcast.5), channel_id=1, replica_groups=mesh['tm'=32,'scen'=16] {'tm'}, dimensions={0} | all-to-all | bytes 2359296 | tf_op jit(solution)/shard_map/all_to_all | solution.py:348
  71.0 1.2 %shard_map.72 = (f32[192,1024]{1,0:T(8,128)}, f32[96,1024]{1,0:T(8,128)}) custom-call(f32[32,72,128]{2,1,0:T(8,128)S(1)} %all_to_all.16.r_ref), custom_call_target="tpu_custom_call" | custom-call | flops 1000000 | bytes 4000000 | tf_op jit(solution)/shard_map/pallas_call | solution.py:349
Async XLA Ops:
  0.6 10.8 %copy-start.2 = (f32[32,96]{1,0:T(8,128)S(1)}, f32[32,96]{1,0:T(8,128)}, u32[]{:S(2)}) copy-start(f32[32,96]{1,0:T(8,128)} %d_ref.1) | copy-start | bytes 36868
  0.6 10.8 %copy-start.3 = (f32[32,48]{1,0:T(8,128)S(1)}, f32[32,48]{1,0:T(8,128)}, u32[]{:S(2)}) copy-start(f32[32,48]{1,0:T(8,128)} %f_ref.1) | copy-start | bytes 18436
  0.7 10.8 %copy-start.1 = (f32[32,48,96]{2,1,0:T(8,128)S(1)}, f32[32,48,96]{2,1,0:T(8,128)}, u32[]{:S(2)}) copy-start(f32[32,48,96]{2,1,0:T(8,128)} %k_ref.1) | copy-start | bytes 1769476
  4.3 20.4 %all-to-all-start = ((f32[8,80,128]{2,1,0:T(8,128)}), f32[8,80,128]{2,1,0:T(8,128)S(1)}, u32[]{:S(2)}, u32[]{:S(2)}) async-start(f32[8,80,128]{2,1,0:T(8,128)} %shard_map.68), calls=%async_computation | async-start | bytes 655360 | tf_op jit(solution)/shard_map/all_to_all | solution.py:315
  11.4 1.4 %copy-start = (f32[32,96,96]{2,1,0:T(8,128)S(1)}, f32[32,96,96]{2,1,0:T(8,128)}, u32[]{:S(2)}) copy-start(f32[32,96,96]{2,1,0:T(8,128)} %a_ref.1) | copy-start | bytes 3538948

commit v6 on v5

--- a/solution.py
+++ b/solution.py
@@ -8,6 +8,8 @@
 f32, bf16 = jnp.float32, jnp.bfloat16
 LANES = 128
 LIMIT = 40 * 1024 * 1024
+
+ALONG, ACROSS = (0, 4, 2, 6, 1, 5, 3, 7), (0, 2, 1, 3)
 
 
 def split(x):
@@ -171,11 +173,10 @@
             out_ref[pl.ds(at + turned[k], steps), LANES:] = low[part]
 
 
-def heads_of(r_ref, body):
-    count = r_ref.shape[0]
+def heads_of(r_ref, body, orders):
     return [
-        jnp.concatenate([r_ref[j, body + k : body + k + 1] for j in range(count)], axis=0)
-        for k in range(3)
+        jnp.concatenate([r_ref[j, body + k : body + k + 1] for j in order], axis=0)
+        for k, order in enumerate(orders)
     ]
 
 
@@ -183,7 +184,7 @@
     count, lines, _ = r_ref.shape
     n = maps.shape[1]
     body = lines - 8
-    heads = heads_of(r_ref, body)
+    heads = heads_of(r_ref, body, [range(count), ALONG, ALONG])
     offsets = with_offsets(jnp.zeros((n, n), f32), columns(heads[0][:, :n], n))
     for j in range(count):
         maps[j] = unpacked(r_ref[j, :body], offsets)
@@ -238,8 +239,10 @@
         for p in (0, 1):
             for s in (0, 1):
                 line = s * first + q + p if q < first else 2 * first + s * rest + q + p - first
-                part = value[32 * s : 32 * s + 32, p * LANES : (p + 1) * LANES]
-                out_ref[pl.ds(line, 32, stride=2 * count)] = part
+                for k in range(outer):
+                    own = slice(32 * s + size * k, 32 * s + size * (k + 1))
+                    place = pl.ds(2 * count * ACROSS.index(k) + line, size, stride=2 * count * outer)
+                    out_ref[place] = value[own, p * LANES : (p + 1) * LANES]
 
 
 def order_kernel(r_ref, states_hbm, controls_hbm, tile_ref, sems):
@@ -248,7 +251,9 @@
     cut = states_hbm.shape[0]
     copies = []
     for g in range(8):
-        parts = [r_ref[4 * g + b] for b in range(4)]
+        parts = [
+            r_ref[ALONG.index((4 * g + b) % 8) * 4 + ACROSS.index(g // 2)] for b in range(4)
+        ]
         for a in range(4):
             value = parts[0]
             for b in range(1, 4):
@@ -345,7 +350,14 @@
         [SMEM] + [VMEM] * 3,
         flops=300_000_000,
     )(at_outer, across, before, local)
-    moved = lax.all_to_all(sent.reshape(blocks, lines, LANES), "tm", 0, 0, tiled=True)
+    moved = lax.all_to_all(
+        sent.reshape(blocks, lines, LANES),
+        "tm",
+        0,
+        0,
+        tiled=True,
+        axis_index_groups=[[k * inner + j for j in ALONG for k in ACROSS]],
+    )
     states, controls = call(
         order_kernel,
         [shape((2 * n, blocks * steps), f32), shape((2 * m, blocks * steps), f32)],

time: 72.6 us -> 72.3 us (level)
  no operation moved by 1% of the time
where the time goes in v6:
time: 72.3 us; the launch traced here: 72 us
  blocking collectives  43.4 us (60%)
  Pallas kernels  13.2 us (18%)
  starting transfers between devices  7.1 us (10%)
  waiting for transfers between devices  6.19 us (9%)
  local copies, waits for them, and re-layouts  1.42 us (2%)
    all_to_all x1, blocking collectives, body(): lax.all_to_all(sent.reshape(blocks, lines, LANES), 'tm', 0, 0, tiled=True...  32.8 us
    all_to_all x1, blocking collectives, body(): lax.all_to_all(group, 'tm', 0, 0, tiled=True, axis_index_groups=far)  10.6 us
    all_to_all x1, starting transfers between devices, body(): lax.all_to_all(payload, 'tm', 0, 0, tiled=True, axis_index_groups=near)  7.1 us
    all_to_all x1, waiting for transfers between devices, body(): lax.all_to_all(payload, 'tm', 0, 0, tiled=True, axis_index_groups=near)  6.19 us
    pallas_call x1, Pallas kernels, body(): call(prefix_kernel, shape((rows, 2 * LANES), bf16), [SMEM] + [VMEM] * 4,...  5.65 us
    pallas_call x1, Pallas kernels, body(): call(summary_kernel, shape((inner, 3 * n // 4 + 8, LANES), f32), [HBM] *...  3.63 us
    pallas_call x1, Pallas kernels, body(): call(apply_kernel, shape((blocks * lines, LANES), f32), [SMEM] + [VMEM] *...  1.54 us
  transfers between devices with their start and end apart: 1, of which 1 were waited for; matrix products, arithmetic and copies ran while one was open for 0% of the time, Pallas kernels for 8%

profile of v6, /device:TPU:448, one launch (start us, length us, event | category | flops | bytes accessed | tf_op | source)
XLA Modules:
  0.0 72.0 jit_solution(17638283031099193664)
XLA Ops:
  0.6 0.0 copy-start.2
  0.6 0.0 copy-start.3
  0.7 0.0 copy-start.1
  0.7 3.6 %shard_map.68 = f32[8,80,128]{2,1,0:T(8,128)} custom-call(f32[32,96,96]{2,1,0:T(8,128)} %a_ref.1, f32[32,96]{1,0:T(8,128)} %d_ref.1, f32[2,96]{1,0:T(2,128)} %bitcast.6), custom_call_target="tpu_custom_call" | custom-call | flops 300000000 | bytes 4000000 | tf_op jit(solution)/shard_map/pallas_call | solution.py:306
  4.3 7.1 %all-to-all-start = ((f32[8,80,128]{2,1,0:T(8,128)}), f32[8,80,128]{2,1,0:T(8,128)S(1)}, u32[]{:S(2)}, u32[]{:S(2)}) async-start(f32[8,80,128]{2,1,0:T(8,128)} %shard_map.68), calls=%async_computation | async-start | bytes 655360 | tf_op jit(solution)/shard_map/all_to_all | solution.py:320
  11.4 0.0 copy-done.2
  11.4 0.0 copy-done.3
  11.4 0.0 copy-done.1
  11.4 0.0 copy-start
  11.4 1.4 %copy-done = f32[32,96,96]{2,1,0:T(8,128)S(1)} copy-done((f32[32,96,96]{2,1,0:T(8,128)S(1)}, f32[32,96,96]{2,1,0:T(8,128)}, u32[]{:S(2)}) %copy-start) | copy-done | bytes 1179672
  12.8 5.6 %shard_map.69.maps_ref = bf16[4608,256]{1,0:T(8,128)(2,1)S(1)} custom-call(s32[1]{0:T(128)} %bitcast.1.i_ref, f32[32,96,96]{2,1,0:T(8,128)S(1)} %copy-done, f32[32,96]{1,0:T(8,128)S(1)} %copy-done.2, f32[32,48,96]{2,1,0:T(8,128)S(1)} %copy-done.1, f32[32,48]{1,0:T(8,128)S(1)} %copy-done.3), custom_call_target="tpu_custom_call" | custom-call | flops 500000000 | bytes 4000000 | tf_op jit(solution)/shard_map/pallas_call | solution.py:323
  18.5 6.2 %all-to-all-done.r_ref = f32[8,80,128]{2,1,0:T(8,128)S(1)} async-done(((f32[8,80,128]{2,1,0:T(8,128)}), f32[8,80,128]{2,1,0:T(8,128)S(1)}, u32[]{:S(2)}, u32[]{:S(2)}) %all-to-all-start) | async-done | bytes 327712 | tf_op jit(solution)/shard_map/all_to_all | solution.py:320
  24.7 1.1 %shard_map.70 = (f32[4,112,128]{2,1,0:T(8,128)S(1)}, f32[96,128]{1,0:T(8,128)S(1)}) custom-call(s32[1]{0:T(128)S(6)} %select_n.12.i_ref, f32[8,80,128]{2,1,0:T(8,128)S(1)} %all-to-all-done.r_ref), custom_call_target="tpu_custom_call" | custom-call | flops 150000000 | bytes 4000000 | tf_op jit(solution)/shard_map/pallas_call | solution.py:337
  25.8 10.6 %all_to_all.15.rows_ref = f32[4,112,128]{2,1,0:T(8,128)S(1)} all-to-all(f32[4,112,128]{2,1,0:T(8,128)S(1)} %get-tuple-element.13), channel_id=1, replica_groups={{0,128,256,384},{16,144,272,400},{32,160,288,416},{48,176,304,432},{64,..., dimensions={0} | all-to-all | bytes 458752 | tf_op jit(solution)/shard_map/all_to_all | solution.py:344
  36.4 1.5 %shard_map.71 = f32[2304,128]{1,0:T(8,128)S(1)} custom-call(s32[1]{0:T(128)S(6)} %select_n.13.i_ref, f32[4,112,128]{2,1,0:T(8,128)S(1)} %all_to_all.15.rows_ref, f32[96,128]{1,0:T(8,128)S(1)} %get-tuple-element.14.inner_ref, bf16[4608,256]{1,0:T(8,128)(2,1)S(1)} %shard_map.69.maps_ref), custom_call_target="tpu_custom_call" | custom-call | flops 300000000 | bytes 4000000 | tf_op jit(solution)/shard_map/pallas_call | solution.py:347
  38.0 32.8 %all_to_all.16.r_ref = f32[32,72,128]{2,1,0:T(8,128)S(1)} all-to-all(f32[32,72,128]{2,1,0:T(8,128)S(1)} %bitcast.5), channel_id=1, replica_groups={{0,256,128,384,64,320,192,448,32,288,160,416,96,352,224,480,16,272,144,..., dimensions={0} | all-to-all | bytes 2359296 | tf_op jit(solution)/shard_map/all_to_all | solution.py:353
  70.8 1.2 %shard_map.72 = (f32[192,1024]{1,0:T(8,128)}, f32[96,1024]{1,0:T(8,128)}) custom-call(f32[32,72,128]{2,1,0:T(8,128)S(1)} %all_to_all.16.r_ref), custom_call_target="tpu_custom_call" | custom-call | flops 1000000 | bytes 4000000 | tf_op jit(solution)/shard_map/pallas_call | solution.py:361
Async XLA Ops:
  0.6 10.8 %copy-start.2 = (f32[32,96]{1,0:T(8,128)S(1)}, f32[32,96]{1,0:T(8,128)}, u32[]{:S(2)}) copy-start(f32[32,96]{1,0:T(8,128)} %d_ref.1) | copy-start | bytes 36868
  0.6 10.8 %copy-start.3 = (f32[32,48]{1,0:T(8,128)S(1)}, f32[32,48]{1,0:T(8,128)}, u32[]{:S(2)}) copy-start(f32[32,48]{1,0:T(8,128)} %f_ref.1) | copy-start | bytes 18436
  0.7 10.8 %copy-start.1 = (f32[32,48,96]{2,1,0:T(8,128)S(1)}, f32[32,48,96]{2,1,0:T(8,128)}, u32[]{:S(2)}) copy-start(f32[32,48,96]{2,1,0:T(8,128)} %k_ref.1) | copy-start | bytes 1769476
  4.3 20.4 %all-to-all-start = ((f32[8,80,128]{2,1,0:T(8,128)}), f32[8,80,128]{2,1,0:T(8,128)S(1)}, u32[]{:S(2)}, u32[]{:S(2)}) async-start(f32[8,80,128]{2,1,0:T(8,128)} %shard_map.68), calls=%async_computation | async-start | bytes 655360 | tf_op jit(solution)/shard_map/all_to_all | solution.py:320
  11.4 1.4 %copy-start = (f32[32,96,96]{2,1,0:T(8,128)S(1)}, f32[32,96,96]{2,1,0:T(8,128)}, u32[]{:S(2)}) copy-start(f32[32,96,96]{2,1,0:T(8,128)} %a_ref.1) | copy-start | bytes 3538948
